TPU v7x, 32 devices: a whole 2x2x4 slice. The times are simulated.
32 devices in a mesh: parts: 2 (over x), tile: 16 (over z, y, core).
Axes of the slice: x: 2, y: 2, z: 4, core: 2. Of those that a mesh axis runs over, the one named last changes fastest.
Arguments:
- features: bfloat16 [512, 2560, 128], P(('parts', 'tile')), parts along dimension 0, may hold values from -40 to 40
- links: int32 [512, 2560], P(('parts', 'tile')), parts along dimension 0, may hold values from 0 to 511, as said below
- coarse_links: int32 [128, 640], P(('parts', 'tile')), parts along dimension 0, may hold values from 0 to 511, as said below
- fine_weight: bfloat16 [5, 128, 128], replicated, may hold values from -0.25693506 to 0.25693506
- fine_bias: float32 [128], replicated, may hold values from -1.5 to 1.5
- coarse_weight: bfloat16 [5, 128, 128], replicated, may hold values from -0.25693506 to 0.25693506
- coarse_bias: float32 [128], replicated, may hold values from -1.5 to 1.5
Outputs:
- fine_map: bfloat16 [512, 2560, 128], P(('parts', 'tile')), parts along dimension 0
- coarse_map: bfloat16 [128, 640, 128], P(('parts', 'tile')), parts along dimension 0
- pooled: float32 [256], P('parts'), parts along dimension 0
There are 2 independent parts, one for each index of `parts`. A program takes and returns all parts, laid end to end along the dimension named above; an argument that names none is the same for every part. Nothing has to cross between parts.
Inputs may be any that keep to these rules, and one draw needn't show every extreme that they name: Bits 0..7 of a code mark links to the neighbours in the eight directions of the steps, bit 8 marks a real pixel; higher bits are 0. In every row the real pixels are a leading run of at least 1280 slots (of the pooled map, at least 320), followed by padding in every row. Links join only real pixels within the grid, and a link is set where both pixels are real except that some pixels lack one diagonal link. `coarse_links`: the same rules as for links, on the pooled grid; a pooled pixel is real exactly where the full-resolution pixel at its block's first row and slot is real.
All inputs are finite; a program needn't handle non-finite values.
Results may differ from a plain program's by a relative error of at most 0.017.
Values may be sent and summed in bfloat16 or wider, within the bound.
A program may use at most 256 MiB of HBM per device.

v0:
```python
import jax
import jax.numpy as jnp
from jax import lax
from jax.sharding import PartitionSpec as P

link_steps = ((-1, 0), (1, 0), (0, -1), (0, 1), (-1, -1), (-1, 1), (1, -1), (1, 1))


def padded_2(value, sides, width):
    for axis, dim in sides:
        size, length = (lax.axis_size(axis), value.shape[dim])
        up = [(i, (i + 1) % size) for i in range(size - 1)]
        down = [(j, i) for i, j in up]
        last = lax.slice_in_dim(value, length - width, length, axis=dim)
        first = lax.slice_in_dim(value, 0, width, axis=dim)
        before = lax.ppermute(last, axis, up)
        after = lax.ppermute(first, axis, down)
        value = jnp.concatenate([before, value, after], axis=dim)
    return value


def neighbour_mean(padded, link_codes, row_count):
    col_count = link_codes.shape[1]
    wide_rows = jnp.pad(padded, ((0, 0), (1, 1), (0, 0)))
    running = jnp.zeros((row_count, col_count, padded.shape[2]), jnp.float32)
    degree = jnp.zeros((row_count, col_count), jnp.float32)
    for bit_index, (row_step, col_step) in enumerate(link_steps):
        link_flag = (link_codes >> bit_index & 1).astype(jnp.float32)
        shifted = wide_rows[
            1 + row_step : 1 + row_step + row_count, 1 + col_step : 1 + col_step + col_count
        ]
        running = running + link_flag[:, :, None] * shifted.astype(jnp.float32)
        degree = degree + link_flag
    return -running / jnp.maximum(degree, 1.0)[:, :, None]


def project(term_rows, weight_slab):
    flattened = term_rows.reshape(-1, term_rows.shape[-1])
    product = jnp.dot(flattened, weight_slab, preferred_element_type=jnp.float32)
    return product.reshape(term_rows.shape[:-1] + (weight_slab.shape[1],))


def real_of(link_codes):
    return (link_codes >> 8 & 1).astype(jnp.float32)[:, :, None]


def layer_output(mixed_sum, bias_row, real_mask):
    return (real_mask * jax.nn.relu(mixed_sum + bias_row)).astype(jnp.bfloat16)


def chebyshev_layer(field_in, link_codes, weights, bias_row, extend):
    row_count = field_in.shape[0]
    real_mask = real_of(link_codes)
    mixed_sum = project(field_in, weights[0])
    current = field_in
    previous = field_in
    for order_index in range(1, weights.shape[0]):
        image_term = neighbour_mean(extend(current), link_codes, row_count)
        if order_index == 1:
            fresh_term = real_mask * image_term
        else:
            fresh_term = real_mask * (2.0 * image_term - previous.astype(jnp.float32))
        fresh_term = fresh_term.astype(jnp.bfloat16)
        mixed_sum = mixed_sum + project(fresh_term, weights[order_index])
        previous, current = (current, fresh_term)
    return layer_output(mixed_sum, bias_row, real_mask)


def pool_pairs(grid):
    row_count, col_count, width_count = grid.shape
    blocks = grid.astype(jnp.float32).reshape(row_count // 2, 2, col_count // 2, 2, width_count)
    return jnp.mean(blocks, axis=(1, 3)).astype(jnp.bfloat16)


def on_device(features, links, coarse_links, fine_weight, fine_bias, coarse_weight, coarse_bias):

    def fine_extend(values):
        return padded_2(values, (("tile", 0),), 1)

    fine_map = chebyshev_layer(features, links, fine_weight, fine_bias, fine_extend)
    coarse_in = pool_pairs(pool_pairs(fine_map))

    def coarse_extend(values):
        return padded_2(values, (("tile", 0),), 1)

    coarse_map = chebyshev_layer(coarse_in, coarse_links, coarse_weight, coarse_bias, coarse_extend)
    column_sums = jnp.sum(coarse_map, axis=(0, 1), dtype=jnp.float32)
    real_count = jnp.sum((coarse_links >> 8 & 1).astype(jnp.float32))
    totals, counted = lax.psum((column_sums, real_count), "tile")
    pooled = totals / counted
    return (fine_map, coarse_map, pooled)


def solution(mesh):
    return jax.shard_map(
        on_device,
        mesh=mesh,
        in_specs=(
            P(("parts", "tile"), None, None),
            P(("parts", "tile"), None),
            P(("parts", "tile"), None),
            P(),
            P(),
            P(),
            P(),
        ),
        out_specs=(P(("parts", "tile"), None, None), P(("parts", "tile"), None, None), P("parts")),
        check_vma=False,
    )
```

profile of v0, /device:TPU:0, one launch (start us, length us, event | category | flops | bytes accessed | tf_op | source)
XLA Modules:
  0.0 531.9 jit_solution(14194819479688930771)
XLA Ops:
  0.6 1.4 fusion.40
  2.0 2.4 collective-permute-start
  4.4 1.3 collective-permute-start.1
  5.7 1.3 and_convert_fusion.17
  7.1 1.9 fusion.36
  9.0 1.2 and_convert_fusion.8
  10.2 0.0 copy-start.6
  10.2 0.0 slice-start.1
  10.3 11.8 %fusion.20 = f32[16,2560,128]{2,1,0:T(8,128)} fusion(bf16[16,2560,128]{2,1,0:T(8,128)(2,1)} %param.7, bf16[5,128,128]{2,1,0:T(8,128)(2,1)} %param.10), kind=kOutput, calls=%fused_computation.84 | convolution fusion | flops 1342177280 | bytes 31490048 | tf_op jit(solution)/shard_map/dot_general | solution.py:39
  22.0 0.2 add_maximum_fusion
  22.2 0.8 copy-done
  23.1 7.3 %select_maximum_fusion.6 = bf16[18,2562,128]{2,1,0:T(8,128)(2,1)S(1)} fusion(bf16[1,2560,128]{2,1,0:T(8,128)(2,1)} %collective-permute-done.1, bf16[16,2560,128]{2,1,0:T(8,128)(2,1)S(1)} %bitcast.58, bf16[1,2560,128]{2,1,0:T(8,128)(2,1)} %copy-done), kind=kLoop, calls=%fused_computation.15 | loop fusion | flops 70834176 | bytes 23602176 | tf_op jit(solution)/shard_map/concatenate | solution.py:18
  30.4 60.0 %multiply_convert_fusion.4 = bf16[16,2560,128]{2,1,0:T(8,128)(2,1)S(1)} fusion(bf16[18,2562,128]{2,1,0:T(8,128)(2,1)S(1)} %select_maximum_fusion.6, bf16[1,2560,128]{2,1,0:T(8,128)(2,1)} %collective-permute-done.1, bf16[16,2560,128]{2,1,0:T(8,128)(2,1)} %param.7, bf16[1,2560,128]{2,1,0:T(8,128)(2,1)S(1)} %copy-done.1, f32[16,2560]{1,0:T(8,128)S(1)} %add_maximum_fusion, ...), kind=kLoop, calls=%fused_computation.8 | loop fusion | flops 152043520 | bytes 86835200 | tf_op jit(solution)/shard_map/convert_element_type | solution.py:63
  90.5 0.1 fusion.39
  90.6 5.2 collective-permute-start.2
  95.8 1.3 collective-permute-start.3
  97.1 8.5 %fusion.18 = f32[16,2560,128]{2,1,0:T(8,128)} fusion(bf16[16,2560,128]{2,1,0:T(8,128)(2,1)S(1)} %multiply_convert_fusion.4, bf16[5,128,128]{2,1,0:T(8,128)(2,1)S(1)} %copy-done.17), kind=kOutput, calls=%fused_computation.82 | convolution fusion | flops 1342177280 | bytes 31490048 | tf_op jit(solution)/shard_map/dot_general | solution.py:39
  105.6 0.8 copy-done.4
  106.4 7.3 %select_maximum_fusion.4 = bf16[18,2562,128]{2,1,0:T(8,128)(2,1)S(1)} fusion(bf16[1,2560,128]{2,1,0:T(8,128)(2,1)} %collective-permute-done.3, bf16[16,2560,128]{2,1,0:T(8,128)(2,1)S(1)} %multiply_convert_fusion.4, bf16[1,2560,128]{2,1,0:T(8,128)(2,1)} %copy-done.4), kind=kLoop, calls=%fused_computation.13 | loop fusion | flops 70834176 | bytes 23602176 | tf_op jit(solution)/shard_map/concatenate | solution.py:18
  113.8 60.1 %multiply_convert_fusion.3 = bf16[16,2560,128]{2,1,0:T(8,128)(2,1)} fusion(bf16[16,2560,128]{2,1,0:T(8,128)(2,1)} %param.7, bf16[18,2562,128]{2,1,0:T(8,128)(2,1)S(1)} %select_maximum_fusion.4, bf16[1,2560,128]{2,1,0:T(8,128)(2,1)} %collective-permute-done.3, bf16[16,2560,128]{2,1,0:T(8,128)(2,1)S(1)} %multiply_convert_fusion.4, ...), kind=kLoop, calls=%fused_computation.7 | loop fusion | flops 167772160 | bytes 97320960 | tf_op jit(solution)/shard_map/convert_element_type | solution.py:63
  173.8 1.4 fusion.38
  175.2 8.3 %collective-permute-start.4 = (bf16[1,2560,128]{2,1,0:T(8,128)(2,1)S(1)}, bf16[1,2560,128]{2,1,0:T(8,128)(2,1)S(1)}, u32[]{:S(2)}, u32[]{:S(2)}) collective-permute-start(bf16[1,2560,128]{2,1,0:T(8,128)(2,1)S(1)} %get-tuple-element.7), channel_id=1, source_target_pairs={{0,1},{1,2},{2,3},{3,4},{4,5},{5,6},{6,7},{7,8},{8,9},{9,10},{10,1... | collective-permute-start | bytes 1966088 | tf_op jit(solution)/shard_map/ppermute | solution.py:16
  183.5 1.5 collective-permute-start.5
  185.0 11.1 %fusion.16 = f32[16,2560,128]{2,1,0:T(8,128)} fusion(bf16[16,2560,128]{2,1,0:T(8,128)(2,1)} %multiply_convert_fusion.3, bf16[5,128,128]{2,1,0:T(8,128)(2,1)S(1)} %copy-done.17), kind=kOutput, calls=%fused_computation.80 | convolution fusion | flops 1342177280 | bytes 31490048 | tf_op jit(solution)/shard_map/dot_general | solution.py:39
  196.1 0.8 copy-done.2
  196.9 9.0 %select_maximum_fusion.2 = bf16[18,2562,128]{2,1,0:T(8,128)(2,1)S(1)} fusion(bf16[1,2560,128]{2,1,0:T(8,128)(2,1)} %collective-permute-done.5, bf16[16,2560,128]{2,1,0:T(8,128)(2,1)} %multiply_convert_fusion.3, bf16[1,2560,128]{2,1,0:T(8,128)(2,1)} %copy-done.2), kind=kLoop, calls=%fused_computation.11 | loop fusion | flops 70834176 | bytes 23602176 | tf_op jit(solution)/shard_map/concatenate | solution.py:18
  206.0 60.4 %multiply_convert_fusion.2 = bf16[16,2560,128]{2,1,0:T(8,128)(2,1)} fusion(bf16[16,2560,128]{2,1,0:T(8,128)(2,1)S(1)} %multiply_convert_fusion.4, bf16[18,2562,128]{2,1,0:T(8,128)(2,1)S(1)} %select_maximum_fusion.2, bf16[1,2560,128]{2,1,0:T(8,128)(2,1)} %collective-permute-done.5, bf16[16,2560,128]{2,1,0:T(8,128)(2,1)} %multiply_convert_fusion.3, ...), kind=kLoop, calls=%fused_computation.6 | loop fusion | flops 167772160 | bytes 97320960 | tf_op jit(solution)/shard_map/convert_element_type | solution.py:63
  266.4 2.4 fusion.37
  268.8 6.4 %collective-permute-start.6 = (bf16[1,2560,128]{2,1,0:T(8,128)(2,1)}, bf16[1,2560,128]{2,1,0:T(8,128)(2,1)S(1)}, u32[]{:S(2)}, u32[]{:S(2)}) collective-permute-start(bf16[1,2560,128]{2,1,0:T(8,128)(2,1)} %get-tuple-element.5), channel_id=1, source_target_pairs={{0,1},{1,2},{2,3},{3,4},{4,5},{5,6},{6,7},{7,8},{8,9},{9,10},{10,1... | collective-permute-start | bytes 1966088 | tf_op jit(solution)/shard_map/ppermute | solution.py:16
  275.2 1.6 collective-permute-start.7
  276.8 0.0 slice-start.4
  276.8 13.2 %fusion.14 = f32[16,2560,128]{2,1,0:T(8,128)} fusion(bf16[16,2560,128]{2,1,0:T(8,128)(2,1)} %multiply_convert_fusion.2, bf16[5,128,128]{2,1,0:T(8,128)(2,1)S(1)} %copy-done.17), kind=kOutput, calls=%fused_computation.78 | convolution fusion | flops 1342177280 | bytes 31490048 | tf_op jit(solution)/shard_map/dot_general | solution.py:39
  290.1 9.8 %select_maximum_fusion = bf16[18,2562,128]{2,1,0:T(8,128)(2,1)S(1)} fusion(bf16[1,2560,128]{2,1,0:T(8,128)(2,1)S(1)} %collective-permute-done.7, bf16[16,2560,128]{2,1,0:T(8,128)(2,1)S(1)} %bitcast.62, bf16[1,2560,128]{2,1,0:T(8,128)(2,1)S(1)} %collective-permute-done.6), kind=kLoop, calls=%fused_computation.9 | loop fusion | flops 70834176 | bytes 23602176 | tf_op jit(solution)/shard_map/concatenate | solution.py:18
  299.9 75.9 %multiply_convert_fusion = bf16[16,2560,128]{2,1,0:T(8,128)(2,1)} fusion(f32[16,2560,128]{2,1,0:T(8,128)} %fusion.14, f32[16,2560,128]{2,1,0:T(8,128)} %fusion.16, f32[16,2560,128]{2,1,0:T(8,128)} %fusion.20, f32[16,2560,128]{2,1,0:T(8,128)} %fusion.18, f32[128]{0:T(128)S(1)} %copy-done.19, f32[16,2560]{1,0:T(8,128)S(1)} %get-tuple-element.21, ...), kind=kOutput, calls=%fused_computation.4 | convolution fusion | flops 1551892480 | bytes 181404160 | tf_op jit(solution)/shard_map/dot_general | solution.py:39
  375.8 57.8 %convert_reduce_fusion = f32[8,1280,128]{2,1,0:T(8,128)} fusion(bf16[8,2,1280,2,128]{4,3,2,1,0:T(2,128)(2,1)} %bitcast.63), kind=kLoop, calls=%fused_computation.3 | loop fusion | flops 9175040 | bytes 15728640 | tf_op jit(solution)/shard_map/reduce_sum | solution.py:72
  433.7 3.1 multiply_convert_fusion.8
  436.8 4.3 convert_reduce_fusion.1
  441.1 0.1 multiply_convert_fusion.13
  441.3 4.6 collective-permute-start.8
  445.8 1.3 collective-permute-start.9
  447.1 0.3 fusion.11
  447.5 3.5 collective-permute-done.9
  451.0 0.3 select_maximum_fusion.14
  451.4 4.1 multiply_convert_fusion.12
  455.5 5.8 %collective-permute-start.10 = (bf16[1,640,128]{2,1,0:T(8,128)(2,1)S(1)}, bf16[1,640,128]{2,1,0:T(8,128)(2,1)S(1)}, u32[]{:S(2)}, u32[]{:S(2)}) collective-permute-start(bf16[1,640,128]{2,1,0:T(8,128)(2,1)S(1)} %get-tuple-element.17), channel_id=1, source_target_pairs={{0,1},{1,2},{2,3},{3,4},{4,5},{5,6},{6,7},{7,8},{8,9},{9,10},{10,1... | collective-permute-start | bytes 491528 | tf_op jit(solution)/shard_map/ppermute | solution.py:16
  461.3 1.3 collective-permute-start.11
  462.6 0.3 convolution_add_fusion.3
  462.9 1.7 collective-permute-done.11
  464.6 0.3 select_maximum_fusion.12
  464.8 4.1 multiply_convert_fusion.11
  469.0 5.3 collective-permute-start.12
  474.3 1.3 collective-permute-start.13
  475.6 0.3 convolution_add_fusion.2
  475.9 1.7 collective-permute-done.13
  477.6 0.3 select_maximum_fusion.10
  477.9 4.1 multiply_convert_fusion.10
  482.0 5.3 collective-permute-start.14
  487.3 1.3 collective-permute-start.15
  488.6 0.3 convolution_add_fusion.1
  488.9 1.7 collective-permute-done.15
  490.6 0.3 select_maximum_fusion.8
  490.9 5.9 %convert_reduce_fusion.2 = (f32[128]{0:T(128)S(1)}, bf16[4,640,128]{2,1,0:T(8,128)(2,1)}) fusion(f32[128]{0:T(128)S(1)} %copy-done.20, f32[4,640,128]{2,1,0:T(8,128)S(1)} %convolution_add_fusion.1, bf16[5,128,128]{2,1,0:T(8,128)(2,1)S(1)} %copy-done.18, bf16[4,640,128]{2,1,0:T(8,128)(2,1)S(1)} %multiply_convert_fusion.11, ...), kind=kOutput, calls=%fused_computation.39 | convolution fusion | flops 96665472 | bytes 7683072 | tf_op jit(solution)/shard_map/dot_general | solution.py:39
  496.7 34.1 %all-reduce.8 = (f32[128]{0:T(128)S(1)}, f32[]{:T(128)}) all-reduce(f32[128]{0:T(128)S(1)} %get-tuple-element.41, f32[]{:T(128)} %get-tuple-element.30), channel_id=1, replica_groups=mesh['parts'=2,'tile'=16] {'tile'}, use_global_device_ids=true, to_apply=%region_3.4 | all-reduce | flops 129 | bytes 1032 | tf_op jit(solution)/shard_map/psum | solution.py:89
  530.8 1.1 broadcast_divide_fusion
  (73 shorter events, 0.2 us)
Async XLA Ops:
  2.0 20.2 %collective-permute-start = (bf16[1,2560,128]{2,1,0:T(8,128)(2,1)S(1)}, bf16[1,2560,128]{2,1,0:T(8,128)(2,1)S(1)}, u32[]{:S(2)}, u32[]{:S(2)}) collective-permute-start(bf16[1,2560,128]{2,1,0:T(8,128)(2,1)S(1)} %get-tuple-element.11), channel_id=1, source_target_pairs={{0,1},{1,2},{2,3},{3,4},{4,5},{5,6},{6,7},{7,8},{8,9},{9,10},{10,1... | collective-permute-start | bytes 1966088 | tf_op jit(solution)/shard_map/ppermute | solution.py:16
  4.4 18.7 %collective-permute-start.1 = (bf16[1,2560,128]{2,1,0:T(8,128)(2,1)S(1)}, bf16[1,2560,128]{2,1,0:T(8,128)(2,1)}, u32[]{:S(2)}, u32[]{:S(2)}) collective-permute-start(bf16[1,2560,128]{2,1,0:T(8,128)(2,1)S(1)} %get-tuple-element.12), channel_id=1, source_target_pairs={{1,0},{2,1},{3,2},{4,3},{5,4},{6,5},{7,6},{8,7},{9,8},{10,9},{11,1... | collective-permute-start | bytes 1966088 | tf_op jit(solution)/shard_map/ppermute | solution.py:17
  9.0 14.1 %slice-start = ((s8[10485760]{0:T(1024)(128)(4,1)}), s8[4194304]{0:T(1024)(128)(4,1)S(1)}, s32[]{:S(2)}) async-start(s8[10485760]{0:T(1024)(128)(4,1)} %bitcast.57), calls=%async_computation | async-start | bytes 8388608
  10.2 11.8 %copy-start.6 = (s32[16,2560]{1,0:T(8,128)S(1)}, s32[16,2560]{1,0:T(8,128)}, u32[]{:S(2)}) copy-start(s32[16,2560]{1,0:T(8,128)} %param.8) | copy-start | bytes 491524
  10.2 12.8 %slice-start.1 = ((s8[10485760]{0:T(1024)(128)(4,1)}), s8[4194304]{0:T(1024)(128)(4,1)S(1)}, s32[]{:S(2)}) async-start(s8[10485760]{0:T(1024)(128)(4,1)} %bitcast.57), calls=%async_computation.1 | async-start | bytes 8388608
  10.3 12.8 %slice-start.2 = ((s8[10485760]{0:T(1024)(128)(4,1)}), s8[2097152]{0:T(1024)(128)(4,1)S(1)}, s32[]{:S(2)}) async-start(s8[10485760]{0:T(1024)(128)(4,1)} %bitcast.57), calls=%async_computation.2 | async-start | bytes 4194304
  22.2 0.8 copy-start
  23.1 7.3 %copy-start.1 = (bf16[1,2560,128]{2,1,0:T(8,128)(2,1)S(1)}, bf16[1,2560,128]{2,1,0:T(8,128)(2,1)}, u32[]{:S(2)}) copy-start(bf16[1,2560,128]{2,1,0:T(8,128)(2,1)} %copy-done) | copy-start | bytes 1966084
  30.4 66.6 %copy-start.17 = (bf16[5,128,128]{2,1,0:T(8,128)(2,1)S(1)}, bf16[5,128,128]{2,1,0:T(8,128)(2,1)}, u32[]{:S(2)}) copy-start(bf16[5,128,128]{2,1,0:T(8,128)(2,1)} %param.10) | copy-start | bytes 491524
  90.6 15.0 %collective-permute-start.2 = (bf16[1,2560,128]{2,1,0:T(8,128)(2,1)S(1)}, bf16[1,2560,128]{2,1,0:T(8,128)(2,1)S(1)}, u32[]{:S(2)}, u32[]{:S(2)}) collective-permute-start(bf16[1,2560,128]{2,1,0:T(8,128)(2,1)S(1)} %get-tuple-element.9), channel_id=1, source_target_pairs={{0,1},{1,2},{2,3},{3,4},{4,5},{5,6},{6,7},{7,8},{8,9},{9,10},{10,1... | collective-permute-start | bytes 1966088 | tf_op jit(solution)/shard_map/ppermute | solution.py:16
  95.8 10.7 %collective-permute-start.3 = (bf16[1,2560,128]{2,1,0:T(8,128)(2,1)S(1)}, bf16[1,2560,128]{2,1,0:T(8,128)(2,1)}, u32[]{:S(2)}, u32[]{:S(2)}) collective-permute-start(bf16[1,2560,128]{2,1,0:T(8,128)(2,1)S(1)} %get-tuple-element.10), channel_id=1, source_target_pairs={{1,0},{2,1},{3,2},{4,3},{5,4},{6,5},{7,6},{8,7},{9,8},{10,9},{11,1... | collective-permute-start | bytes 1966088 | tf_op jit(solution)/shard_map/ppermute | solution.py:17
  105.6 0.8 copy-start.4
  106.4 7.3 %copy-start.5 = (bf16[1,2560,128]{2,1,0:T(8,128)(2,1)S(1)}, bf16[1,2560,128]{2,1,0:T(8,128)(2,1)}, u32[]{:S(2)}) copy-start(bf16[1,2560,128]{2,1,0:T(8,128)(2,1)} %copy-done.4) | copy-start | bytes 1966084
  175.2 20.9 %collective-permute-start.4 = (bf16[1,2560,128]{2,1,0:T(8,128)(2,1)S(1)}, bf16[1,2560,128]{2,1,0:T(8,128)(2,1)S(1)}, u32[]{:S(2)}, u32[]{:S(2)}) collective-permute-start(bf16[1,2560,128]{2,1,0:T(8,128)(2,1)S(1)} %get-tuple-element.7), channel_id=1, source_target_pairs={{0,1},{1,2},{2,3},{3,4},{4,5},{5,6},{6,7},{7,8},{8,9},{9,10},{10,1... | collective-permute-start | bytes 1966088 | tf_op jit(solution)/shard_map/ppermute | solution.py:16
  183.5 13.4 %collective-permute-start.5 = (bf16[1,2560,128]{2,1,0:T(8,128)(2,1)S(1)}, bf16[1,2560,128]{2,1,0:T(8,128)(2,1)}, u32[]{:S(2)}, u32[]{:S(2)}) collective-permute-start(bf16[1,2560,128]{2,1,0:T(8,128)(2,1)S(1)} %get-tuple-element.8), channel_id=1, source_target_pairs={{1,0},{2,1},{3,2},{4,3},{5,4},{6,5},{7,6},{8,7},{9,8},{10,9},{11,1... | collective-permute-start | bytes 1966088 | tf_op jit(solution)/shard_map/ppermute | solution.py:17
  196.1 0.8 copy-start.2
  196.9 9.0 %copy-start.3 = (bf16[1,2560,128]{2,1,0:T(8,128)(2,1)S(1)}, bf16[1,2560,128]{2,1,0:T(8,128)(2,1)}, u32[]{:S(2)}) copy-start(bf16[1,2560,128]{2,1,0:T(8,128)(2,1)} %copy-done.2) | copy-start | bytes 1966084
  268.8 21.2 %collective-permute-start.6 = (bf16[1,2560,128]{2,1,0:T(8,128)(2,1)}, bf16[1,2560,128]{2,1,0:T(8,128)(2,1)S(1)}, u32[]{:S(2)}, u32[]{:S(2)}) collective-permute-start(bf16[1,2560,128]{2,1,0:T(8,128)(2,1)} %get-tuple-element.5), channel_id=1, source_target_pairs={{0,1},{1,2},{2,3},{3,4},{4,5},{5,6},{6,7},{7,8},{8,9},{9,10},{10,1... | collective-permute-start | bytes 1966088 | tf_op jit(solution)/shard_map/ppermute | solution.py:16
  275.2 14.9 %slice-start.6 = ((s8[10485760]{0:T(1024)(128)(4,1)}), s8[4194304]{0:T(1024)(128)(4,1)S(1)}, s32[]{:S(2)}) async-start(s8[10485760]{0:T(1024)(128)(4,1)} %bitcast.61), calls=%async_computation.6 | async-start | bytes 8388608
  275.2 14.9 %slice-start.7 = ((s8[10485760]{0:T(1024)(128)(4,1)}), s8[4194304]{0:T(1024)(128)(4,1)S(1)}, s32[]{:S(2)}) async-start(s8[10485760]{0:T(1024)(128)(4,1)} %bitcast.61), calls=%async_computation.7 | async-start | bytes 8388608
  275.2 14.9 %slice-start.8 = ((s8[10485760]{0:T(1024)(128)(4,1)}), s8[2097152]{0:T(1024)(128)(4,1)S(1)}, s32[]{:S(2)}) async-start(s8[10485760]{0:T(1024)(128)(4,1)} %bitcast.61), calls=%async_computation.8 | async-start | bytes 4194304
  275.2 14.8 %collective-permute-start.7 = (bf16[1,2560,128]{2,1,0:T(8,128)(2,1)}, bf16[1,2560,128]{2,1,0:T(8,128)(2,1)S(1)}, u32[]{:S(2)}, u32[]{:S(2)}) collective-permute-start(bf16[1,2560,128]{2,1,0:T(8,128)(2,1)} %get-tuple-element.6), channel_id=1, source_target_pairs={{1,0},{2,1},{3,2},{4,3},{5,4},{6,5},{7,6},{8,7},{9,8},{10,9},{11,1... | collective-permute-start | bytes 1966088 | tf_op jit(solution)/shard_map/ppermute | solution.py:17
  276.8 23.1 %slice-start.3 = ((s8[10485760]{0:T(1024)(128)(4,1)}), s8[4194304]{0:T(1024)(128)(4,1)S(1)}, s32[]{:S(2)}) async-start(s8[10485760]{0:T(1024)(128)(4,1)} %bitcast.59), calls=%async_computation.3 | async-start | bytes 8388608
  276.8 23.1 %slice-start.4 = ((s8[10485760]{0:T(1024)(128)(4,1)}), s8[2097152]{0:T(1024)(128)(4,1)S(1)}, s32[]{:S(2)}) async-start(s8[10485760]{0:T(1024)(128)(4,1)} %bitcast.59), calls=%async_computation.4 | async-start | bytes 4194304
  290.0 9.9 %slice-start.5 = ((s8[10485760]{0:T(1024)(128)(4,1)}), s8[4194304]{0:T(1024)(128)(4,1)S(1)}, s32[]{:S(2)}) async-start(s8[10485760]{0:T(1024)(128)(4,1)} %bitcast.59), calls=%async_computation.5 | async-start | bytes 8388608
  290.0 9.9 %copy-start.19 = (f32[128]{0:T(128)S(1)}, f32[128]{0:T(128)}, u32[]{:S(2)}) copy-start(f32[128]{0:T(128)} %param.11) | copy-start | bytes 1540
  433.7 13.5 %copy-start.18 = (bf16[5,128,128]{2,1,0:T(8,128)(2,1)S(1)}, bf16[5,128,128]{2,1,0:T(8,128)(2,1)}, u32[]{:S(2)}) copy-start(bf16[5,128,128]{2,1,0:T(8,128)(2,1)} %param.12) | copy-start | bytes 491524
  433.7 17.6 %copy-start.7 = (f32[4,640]{1,0:T(4,128)S(1)}, f32[4,640]{1,0:T(4,128)}, u32[]{:S(2)}) copy-start(f32[4,640]{1,0:T(4,128)} %get-tuple-element.32) | copy-start | bytes 30724
  433.7 17.6 %copy-start.8 = (f32[4,640]{1,0:T(4,128)S(1)}, f32[4,640]{1,0:T(4,128)}, u32[]{:S(2)}) copy-start(f32[4,640]{1,0:T(4,128)} %get-tuple-element.33) | copy-start | bytes 30724
  433.7 17.6 %copy-start.9 = (f32[4,640]{1,0:T(4,128)S(1)}, f32[4,640]{1,0:T(4,128)}, u32[]{:S(2)}) copy-start(f32[4,640]{1,0:T(4,128)} %get-tuple-element.34) | copy-start | bytes 30724
  433.7 17.6 %copy-start.10 = (f32[4,640]{1,0:T(4,128)S(1)}, f32[4,640]{1,0:T(4,128)}, u32[]{:S(2)}) copy-start(f32[4,640]{1,0:T(4,128)} %get-tuple-element.35) | copy-start | bytes 30724
  433.7 17.6 %copy-start.11 = (f32[4,640]{1,0:T(4,128)S(1)}, f32[4,640]{1,0:T(4,128)}, u32[]{:S(2)}) copy-start(f32[4,640]{1,0:T(4,128)} %get-tuple-element.36) | copy-start | bytes 30724
  433.7 17.6 %copy-start.12 = (f32[4,640]{1,0:T(4,128)S(1)}, f32[4,640]{1,0:T(4,128)}, u32[]{:S(2)}) copy-start(f32[4,640]{1,0:T(4,128)} %get-tuple-element.37) | copy-start | bytes 30724
  433.7 17.6 %copy-start.13 = (f32[4,640]{1,0:T(4,128)S(1)}, f32[4,640]{1,0:T(4,128)}, u32[]{:S(2)}) copy-start(f32[4,640]{1,0:T(4,128)} %get-tuple-element.38) | copy-start | bytes 30724
  433.7 17.6 %copy-start.14 = (f32[4,640]{1,0:T(4,128)S(1)}, f32[4,640]{1,0:T(4,128)}, u32[]{:S(2)}) copy-start(f32[4,640]{1,0:T(4,128)} %get-tuple-element.39) | copy-start | bytes 30724
  433.7 17.6 %copy-start.15 = (f32[4,640]{1,0:T(4,128)S(1)}, f32[4,640]{1,0:T(4,128)}, u32[]{:S(2)}) copy-start(f32[4,640]{1,0:T(4,128)} %get-tuple-element.40) | copy-start | bytes 30724
  433.7 17.6 %copy-start.16 = (f32[4,640]{1,0:T(4,128)S(1)}, f32[4,640]{1,0:T(4,128)}, u32[]{:S(2)}) copy-start(f32[4,640]{1,0:T(4,128)} %get-tuple-element.31) | copy-start | bytes 30724
  441.3 6.2 %collective-permute-start.8 = (bf16[1,640,128]{2,1,0:T(8,128)(2,1)S(1)}, bf16[1,640,128]{2,1,0:T(8,128)(2,1)S(1)}, u32[]{:S(2)}, u32[]{:S(2)}) collective-permute-start(bf16[1,640,128]{2,1,0:T(8,128)(2,1)S(1)} %get-tuple-element.19), channel_id=1, source_target_pairs={{0,1},{1,2},{2,3},{3,4},{4,5},{5,6},{6,7},{7,8},{8,9},{9,10},{10,1... | collective-permute-start | bytes 491528 | tf_op jit(solution)/shard_map/ppermute | solution.py:16
  445.8 5.2 collective-permute-start.9
  455.5 7.4 %collective-permute-start.10 = (bf16[1,640,128]{2,1,0:T(8,128)(2,1)S(1)}, bf16[1,640,128]{2,1,0:T(8,128)(2,1)S(1)}, u32[]{:S(2)}, u32[]{:S(2)}) collective-permute-start(bf16[1,640,128]{2,1,0:T(8,128)(2,1)S(1)} %get-tuple-element.17), channel_id=1, source_target_pairs={{0,1},{1,2},{2,3},{3,4},{4,5},{5,6},{6,7},{7,8},{8,9},{9,10},{10,1... | collective-permute-start | bytes 491528 | tf_op jit(solution)/shard_map/ppermute | solution.py:16
  461.3 3.3 collective-permute-start.11
  469.0 21.9 %copy-start.20 = (f32[128]{0:T(128)S(1)}, f32[128]{0:T(128)}, u32[]{:S(2)}) copy-start(f32[128]{0:T(128)} %param.13) | copy-start | bytes 1540
  469.0 6.9 %collective-permute-start.12 = (bf16[1,640,128]{2,1,0:T(8,128)(2,1)S(1)}, bf16[1,640,128]{2,1,0:T(8,128)(2,1)S(1)}, u32[]{:S(2)}, u32[]{:S(2)}) collective-permute-start(bf16[1,640,128]{2,1,0:T(8,128)(2,1)S(1)} %get-tuple-element.15), channel_id=1, source_target_pairs={{0,1},{1,2},{2,3},{3,4},{4,5},{5,6},{6,7},{7,8},{8,9},{9,10},{10,1... | collective-permute-start | bytes 491528 | tf_op jit(solution)/shard_map/ppermute | solution.py:16
  474.3 3.3 collective-permute-start.13
  482.0 6.9 %collective-permute-start.14 = (bf16[1,640,128]{2,1,0:T(8,128)(2,1)S(1)}, bf16[1,640,128]{2,1,0:T(8,128)(2,1)S(1)}, u32[]{:S(2)}, u32[]{:S(2)}) collective-permute-start(bf16[1,640,128]{2,1,0:T(8,128)(2,1)S(1)} %get-tuple-element.13), channel_id=1, source_target_pairs={{0,1},{1,2},{2,3},{3,4},{4,5},{5,6},{6,7},{7,8},{8,9},{9,10},{10,1... | collective-permute-start | bytes 491528 | tf_op jit(solution)/shard_map/ppermute | solution.py:16
  487.3 3.3 collective-permute-start.15
where the time goes:
time: 533 us; the launch traced here: 532 us
  other arithmetic  298 us (56%)
  matrix products  128 us (24%)
  starting transfers between devices  53.9 us (10%)
  blocking collectives  34.1 us (6%)
  waiting for transfers between devices  8.55 us (2%)
  local copies, waits for them, and re-layouts  7.98 us (1%)
    convert_element_type x6, other arithmetic, chebyshev_layer(): fresh_term = fresh_term.astype(jnp.bfloat16)  193 us
    dot_general x10, matrix products, project(): jnp.dot(flattened, weight_slab, preferred_element_type=jnp.float32)  128 us
    reduce_sum x2, other arithmetic, pool_pairs(): return jnp.mean(blocks, axis=(1, 3)).astype(jnp.bfloat16)  62.1 us
    ppermute x8, starting transfers between devices, padded_2(): before = lax.ppermute(last, axis, up)  43.1 us
    concatenate x8, other arithmetic, padded_2(): value = jnp.concatenate([before, value, after], axis=dim)  34.5 us
    psum x1, blocking collectives, on_device(): totals, counted = lax.psum((column_sums, real_count), 'tile')  34.1 us
    ppermute x8, starting transfers between devices, padded_2(): after = lax.ppermute(first, axis, down)  10.8 us
  transfers between devices with their start and end apart: 16, of which 4 were waited for; matrix products, arithmetic and copies ran while one was open for 9% of the time, Pallas kernels for 0%

commit v1 on v0

v1 whole, which is shorter than its diff:
```python
import jax
import jax.numpy as jnp
import numpy as np
from jax import lax
from jax.experimental import pallas as pl
from jax.experimental.pallas import tpu as pltpu
from jax.sharding import PartitionSpec as P

USE = 64
WIN = 80
EDGE = 16
DEEP = 4
link_steps = ((-1, 0), (1, 0), (0, -1), (0, 1), (-1, -1), (-1, 1), (1, -1), (1, 1))


def bit_table():
    table = np.zeros((WIN, 256), np.int32)
    for bit, (dr, dc) in enumerate(link_steps):
        for i in range(WIN):
            table[i, (dr + 1) * WIN + (i + dc) % WIN] = 1 << bit
    return table


def pool_tables():
    first = np.zeros((64, 256), np.float32)
    for row in range(2):
        for col in range(32):
            for dr in range(2):
                for dc in range(2):
                    first[row * 32 + col, (2 * row + dr) * 64 + 2 * col + dc] = 0.25
    second = np.zeros((16, 64), np.float32)
    for col in range(16):
        for dr in range(2):
            for dc in range(2):
                second[col, dr * 32 + 2 * col + dc] = 0.25
    return first, second


def window_kernel(rows, pool, refs):
    (main, left, right, tmain, tleft, tright, bmain, bleft, bright, codes, bits, w01, w23, w4, bias) = refs[:15]
    rest = refs[15:]
    if pool:
        pool1, pool2, _, out, coarse = rest[:5]
        rest = rest[5:]
    else:
        out, sums = rest[:2]
        rest = rest[2:]
    p0, p1, p2, p3, p4, links, coef = rest
    step = pl.program_id(0)
    full = rows + 2 * DEEP

    @pl.when(step == 0)
    def _():
        for ref in (p0, p1, p2, p3, p4):
            ref[...] = jnp.zeros_like(ref)
        if not pool:
            sums[...] = jnp.zeros_like(sums)

    code = codes[0]
    degree = jnp.zeros(code.shape, jnp.int32)
    for bit in range(8):
        degree = degree + ((code >> bit) & 1)
    scale = -2.0 / jnp.maximum(degree.astype(jnp.float32), 1.0)
    real = ((code >> 8) & 1).astype(jnp.float32)
    table = bits[...]
    low = lax.broadcasted_iota(jnp.int32, (EDGE, 128), 0) < 8

    for r in range(full):
        if r < DEEP:
            m, a, b, s = tmain, tleft, tright, r
        elif r < DEEP + rows:
            m, a, b, s = main, left, right, r - DEEP
        else:
            m, a, b, s = bmain, bleft, bright, r - DEEP - rows
        mask = jnp.broadcast_to(real[:, r : r + 1], (WIN, 128))
        side = jnp.where(low, b[s].astype(jnp.float32), a[s].astype(jnp.float32))
        p0[pl.ds(r * WIN, USE), :] = (m[s].astype(jnp.float32) * mask[:USE]).astype(jnp.bfloat16)
        p0[pl.ds(r * WIN + USE, EDGE), :] = (side * mask[USE:]).astype(jnp.bfloat16)
        if 1 <= r < full - 1:
            wide = jnp.broadcast_to(code[:, r : r + 1], (WIN, 256))
            links[r] = jnp.where((wide & table) != 0, 1.0, 0.0).astype(jnp.bfloat16)
            coef[r] = jnp.broadcast_to(scale[:, r : r + 1], (WIN, 128))

    terms = (p0, p1, p2, p3, p4)
    for k in range(1, 5):
        src, dst = terms[k - 1], terms[k]
        for r in range(k, full - k):
            acc = jnp.dot(links[r], src[pl.ds((r - 1) * WIN, 256), :], preferred_element_type=jnp.float32)
            if k == 1:
                fresh = acc * (0.5 * coef[r])
            else:
                fresh = acc * coef[r] - terms[k - 2][pl.ds(r * WIN, WIN), :].astype(jnp.float32)
            dst[pl.ds(r * WIN, WIN), :] = fresh.astype(jnp.bfloat16)

    def gather(ref, first, count):
        return jnp.concatenate([ref[pl.ds((first + j) * WIN, USE), :] for j in range(count)], axis=0)

    group = 4
    for g in range(rows // group):
        first = DEEP + g * group
        q = [gather(t, first, group) for t in terms]
        mixed = jnp.dot(jnp.concatenate([q[0], q[1]], axis=1), w01[...], preferred_element_type=jnp.float32)
        mixed += jnp.dot(jnp.concatenate([q[2], q[3]], axis=1), w23[...], preferred_element_type=jnp.float32)
        mixed += jnp.dot(q[4], w4[...], preferred_element_type=jnp.float32)
        mask = jnp.concatenate(
            [jnp.broadcast_to(real[:USE, first + j : first + j + 1], (USE, 128)) for j in range(group)], axis=0
        )
        res = (mask * jnp.maximum(mixed + bias[...], 0.0)).astype(jnp.bfloat16)
        for j in range(group):
            out[g * group + j] = res[j * USE : (j + 1) * USE]
        if pool:
            half = jnp.dot(pool1[...], res, preferred_element_type=jnp.float32).astype(jnp.bfloat16)
            coarse[g] = jnp.dot(pool2[...], half, preferred_element_type=jnp.float32).astype(jnp.bfloat16)
        else:
            sums[...] += jnp.sum(res.astype(jnp.float32).reshape(-1, 8, 128), axis=0)


def layer(name, main, top, bottom, codes, weights, bias, first, count, pool, canvas=None):
    rows, cols, width = main.shape
    total = cols // USE
    chunked = top.shape[1] != cols
    ratio = USE // EDGE

    def spec(n, pick, size):
        return pl.BlockSpec((n, size, width), lambda w: (0, pick(w), 0))

    def left_of(w):
        return jnp.maximum((first + w) * ratio - 1, 0)

    def right_of(w):
        return jnp.minimum((first + w) * ratio + ratio, total * ratio - 1)

    if chunked:
        halo = [
            spec(DEEP, lambda w: w, USE),
            spec(DEEP, lambda w: jnp.where(w == 0, count * ratio + 1, w * ratio - 1), EDGE),
            spec(DEEP, lambda w: w * ratio + ratio, EDGE),
        ]
    else:
        halo = [spec(DEEP, lambda w: first + w, USE), spec(DEEP, left_of, EDGE), spec(DEEP, right_of, EDGE)]

    def whole(*shape):
        return pl.BlockSpec(shape, lambda w: (0,) * len(shape))

    full = rows + 2 * DEEP
    in_specs = (
        [spec(rows, lambda w: first + w, USE), spec(rows, left_of, EDGE), spec(rows, right_of, EDGE)]
        + halo + halo
        + [pl.BlockSpec((1, WIN, full), lambda w: (first + w, 0, 0))]
        + [whole(WIN, 256), whole(256, 128), whole(256, 128), whole(128, 128), whole(1, 128)]
    )
    operands = [main] * 3 + [top] * 3 + [bottom] * 3 + [codes, jnp.asarray(bit_table())]
    operands += [weights[0:2].reshape(256, 128), weights[2:4].reshape(256, 128), weights[4], bias.reshape(1, 128)]
    out_map = jax.ShapeDtypeStruct((rows, cols, width), jnp.bfloat16)
    aliases = {}
    if pool:
        pool1, pool2 = pool_tables()
        operands += [jnp.asarray(pool1, jnp.bfloat16), jnp.asarray(pool2, jnp.bfloat16)]
        in_specs += [whole(64, 256), whole(16, 64)]
        if canvas is None:
            operands.append(bias.reshape(1, 128))
            in_specs.append(whole(1, 128))
        else:
            aliases = {len(operands): 0}
            operands.append(canvas)
            in_specs.append(pl.BlockSpec(memory_space=pl.ANY))
        out_shape = [out_map, jax.ShapeDtypeStruct((rows // 4, count * USE // 4, width), jnp.bfloat16)]
        out_specs = [spec(rows, lambda w: first + w, USE), spec(rows // 4, lambda w: w, USE // 4)]
    else:
        out_shape = [out_map, jax.ShapeDtypeStruct((8, 128), jnp.float32)]
        out_specs = [spec(rows, lambda w: first + w, USE), whole(8, 128)]
    field = pltpu.VMEM((full * WIN + 16, 128), jnp.bfloat16)
    pixels = full * WIN * count
    return pl.pallas_call(
        lambda *refs: window_kernel(rows, pool, refs),
        grid=(count,),
        in_specs=in_specs,
        out_specs=out_specs,
        out_shape=out_shape,
        input_output_aliases=aliases,
        scratch_shapes=[field] * 5
        + [pltpu.VMEM((full, WIN, 256), jnp.bfloat16), pltpu.VMEM((full, WIN, 128), jnp.float32)],
        compiler_params=pltpu.CompilerParams(vmem_limit_bytes=40 * 2**20),
        cost_estimate=pl.CostEstimate(
            flops=pixels * 128 * 2 * 256 * 4, bytes_accessed=pixels * 128 * 4, transcendentals=0
        ),
        name=name,
    )(*operands)


def shifts():
    size = lax.axis_size("tile")
    up = [(i, i + 1) for i in range(size - 1)]
    down = [(i + 1, i) for i in range(size - 1)]
    return up, down


def code_windows(links):
    up, down = shifts()
    above = lax.ppermute(links[-DEEP:], "tile", up)
    below = lax.ppermute(links[:DEEP], "tile", down)
    codes = jnp.concatenate([above, links, below], axis=0)
    rows, cols = codes.shape
    count = cols // USE
    body = codes.reshape(rows, count, USE)
    after = jnp.pad(codes[:, USE:], ((0, 0), (0, USE))).reshape(rows, count, USE)[:, :, :8]
    before = jnp.pad(codes[:, :-USE], ((0, 0), (USE, 0))).reshape(rows, count, USE)[:, :, USE - 8 :]
    return jnp.concatenate([body, after, before], axis=2).transpose(1, 2, 0)


CHUNKS = (0.1, 0.3, 0.6, 1.0)


def on_device(features, links, coarse_links, fine_weight, fine_bias, coarse_weight, coarse_bias):
    up, down = shifts()
    rows, cols, width = features.shape
    total = cols // USE
    ends = [round(total * f) for f in CHUNKS]
    starts = [0] + ends[:-1]
    fine_codes = code_windows(links)
    coarse_codes = code_windows(coarse_links)
    halos = []
    for lo, hi in zip(starts, ends):
        a, b = lo * USE, hi * USE
        right = min(b, cols - EDGE)
        left = max(a - EDGE, 0)

        def piece(part):
            return jnp.concatenate(
                [part[:, a:b], part[:, right : right + EDGE], part[:, left : left + EDGE]], axis=1
            )

        above = lax.ppermute(piece(features[-DEEP:]), "tile", up)
        below = lax.ppermute(piece(features[:DEEP]), "tile", down)
        halos.append((above, below))
    canvas = None
    mids, tops, bottoms = [], [], []
    for n, (lo, hi) in enumerate(zip(starts, ends)):
        above, below = halos[n]
        canvas, mid = layer(
            f"fine{n}", features, above, below, fine_codes, fine_weight, fine_bias, lo, hi - lo, True, canvas
        )
        mids.append(mid)
        tops.append(lax.ppermute(mid, "tile", up))
        bottoms.append(lax.ppermute(mid, "tile", down))
    coarse_in = jnp.concatenate(mids, axis=1)
    above = jnp.concatenate(tops, axis=1)
    below = jnp.concatenate(bottoms, axis=1)
    coarse_map, sums = layer(
        "coarse", coarse_in, above, below, coarse_codes, coarse_weight, coarse_bias, 0, coarse_in.shape[1] // USE, False
    )
    real_count = jnp.sum((coarse_links >> 8 & 1).astype(jnp.float32))
    totals, counted = lax.psum((jnp.sum(sums, axis=0), real_count), "tile")
    return (canvas, coarse_map, totals / counted)


def solution(mesh):
    return jax.shard_map(
        on_device,
        mesh=mesh,
        in_specs=(
            P(("parts", "tile"), None, None),
            P(("parts", "tile"), None),
            P(("parts", "tile"), None),
            P(),
            P(),
            P(),
            P(),
        ),
        out_specs=(P(("parts", "tile"), None, None), P(("parts", "tile"), None, None), P("parts")),
        check_vma=False,
    )
```

time: 533 us -> 284 us (0.53)
  other arithmetic: 298 us -> 12 us
  Pallas kernels: 0 us -> 155 us
  matrix products: 128 us -> 0 us
  local copies, waits for them, and re-layouts: 7.98 us -> 22.7 us
  waiting for transfers between devices: 8.55 us -> 0.05 us
  starting transfers between devices: 53.9 us -> 59.4 us
    convert_element_type x10 -> x0, other arithmetic: 199 us -> none  [the longest x6 193 us: chebyshev_layer(): fresh_term = fresh_term.astype(jnp.bfloat16)]
    pallas_call x0 -> x5, Pallas kernels: none -> 155 us  [layer(): pl.pallas_call(lambda *refs: window_kernel(rows, pool, refs), grid=(count...]
    dot_general x10 -> x0, matrix products: 128 us -> none  [project(): jnp.dot(flattened, weight_slab, preferred_element_type=jnp.float32)]
    reduce_sum x2 -> x1, other arithmetic: 62.1 us -> 0.02 us  [on_device(): totals, counted = lax.psum((jnp.sum(sums, axis=0), real_count), 'tile')]
    concatenate x8 -> x14, other arithmetic: 34.5 us -> 10.2 us  [the longest x8 6.46 us: piece(): jnp.concatenate([part[:, a:b], part[:, right:right + EDGE], part[:, left:...]
    ppermute x16 -> x20, waiting for transfers between devices: 8.55 us -> 0.05 us  [the longest x4 0.01 us: on_device(): below = lax.ppermute(piece(features[:DEEP]), 'tile', down)]
    ppermute x16 -> x20, starting transfers between devices: 53.9 us -> 59.4 us  [the longest x4 20.7 us: on_device(): tops.append(lax.ppermute(mid, 'tile', up))]
    unnamed x60 -> x46, local copies, waits for them, and re-layouts: 2.63 us -> 7.97 us
  transfers between devices with their start and end apart: 16 -> 20, of which waited for: 4 -> 0; matrix products, arithmetic and copies ran while one was open for 9% -> 9% of each run, Pallas kernels for 0% -> 50%
where the time goes in v1:
time: 284 us; the launch traced here: 283 us
  Pallas kernels  155 us (55%)
  starting transfers between devices  59.4 us (21%)
  blocking collectives  32.4 us (11%)
  local copies, waits for them, and re-layouts  22.7 us (8%)
  other arithmetic  12 us (4%)
    pallas_call x5, Pallas kernels, layer(): pl.pallas_call(lambda *refs: window_kernel(rows, pool, refs), grid=(count...  155 us
    psum x1, blocking collectives, on_device(): totals, counted = lax.psum((jnp.sum(sums, axis=0), real_count), 'tile')  32.4 us
    ppermute x4, starting transfers between devices, on_device(): tops.append(lax.ppermute(mid, 'tile', up))  20.7 us
    ppermute x4, starting transfers between devices, on_device(): above = lax.ppermute(piece(features[-DEEP:]), 'tile', up)  17.8 us
    unnamed x46, local copies, waits for them, and re-layouts  7.97 us
    ppermute x2, starting transfers between devices, code_windows(): above = lax.ppermute(links[-DEEP:], 'tile', up)  7.66 us
    concatenate x8, other arithmetic, piece(): jnp.concatenate([part[:, a:b], part[:, right:right + EDGE], part[:, left:...  6.46 us
  transfers between devices with their start and end apart: 20, of which 0 were waited for; matrix products, arithmetic and copies ran while one was open for 9% of the time, Pallas kernels for 50%

profile of v1, /device:TPU:0, one launch (start us, length us, event | category | flops | bytes accessed | tf_op | source)
XLA Modules:
  0.0 283.0 jit_solution(9688651337989109121)
XLA Ops:
  0.6 2.5 collective-permute-start.18
  3.1 1.3 collective-permute-start.19
  4.4 0.9 fusion.8
  5.4 5.2 %collective-permute-start.2 = (s32[4,2560]{1,0:T(4,128)S(1)}, s32[4,2560]{1,0:T(4,128)S(1)}, u32[]{:S(2)}, u32[]{:S(2)}) collective-permute-start(s32[4,2560]{1,0:T(4,128)S(1)} %get-tuple-element.49), channel_id=1, source_target_pairs={{0,1},{1,2},{2,3},{3,4},{4,5},{5,6},{6,7},{7,8},{8,9},{9,10},{10,1... | collective-permute-start | bytes 122888 | tf_op jit(solution)/shard_map/ppermute | solution.py:200
  10.6 1.3 collective-permute-start.3
  11.9 0.9 fusion.1
  12.8 1.1 fusion
  13.9 4.3 %collective-permute-start.8 = (bf16[4,288,128]{2,1,0:T(8,128)(2,1)S(1)}, bf16[4,288,128]{2,1,0:T(8,128)(2,1)S(1)}, u32[]{:S(2)}, u32[]{:S(2)}) collective-permute-start(bf16[4,288,128]{2,1,0:T(8,128)(2,1)S(1)} %pad_maximum_fusion.9), channel_id=1, source_target_pairs={{0,1},{1,2},{2,3},{3,4},{4,5},{5,6},{6,7},{7,8},{8,9},{9,10},{10,1... | collective-permute-start | bytes 884744 | tf_op jit(solution)/shard_map/ppermute | solution.py:233
  18.2 1.3 fusion.2
  19.5 1.5 fusion.3
  21.0 1.7 fusion.4
  22.8 0.7 fusion.6
  23.4 0.6 slice_bitcast_fusion.refs_13_
  24.0 0.7 pad_maximum_fusion.10
  24.8 0.8 pad_maximum_fusion.7
  25.6 0.8 pad_maximum_fusion.8
  26.5 0.9 pad_maximum_fusion.2
  27.4 0.9 pad_maximum_fusion.3
  28.4 1.1 pad_maximum_fusion.1
  29.4 1.1 pad_maximum_fusion
  30.5 0.6 convert_reduce_fusion
  31.1 1.3 collective-permute-start.9
  32.4 5.1 %collective-permute-start.6 = (bf16[4,544,128]{2,1,0:T(8,128)(2,1)}, bf16[4,544,128]{2,1,0:T(8,128)(2,1)}, u32[]{:S(2)}, u32[]{:S(2)}) collective-permute-start(bf16[4,544,128]{2,1,0:T(8,128)(2,1)} %pad_maximum_fusion.7), channel_id=1, source_target_pairs={{0,1},{1,2},{2,3},{3,4},{4,5},{5,6},{6,7},{7,8},{8,9},{9,10},{10,1... | collective-permute-start | bytes 1671176 | tf_op jit(solution)/shard_map/ppermute | solution.py:233
  37.5 0.6 pad_add_fusion.2
  38.1 1.3 collective-permute-start.7
  39.4 3.5 %collective-permute-start.4 = (bf16[4,800,128]{2,1,0:T(8,128)(2,1)}, bf16[4,800,128]{2,1,0:T(8,128)(2,1)S(1)}, u32[]{:S(2)}, u32[]{:S(2)}) collective-permute-start(bf16[4,800,128]{2,1,0:T(8,128)(2,1)} %pad_maximum_fusion.2), channel_id=1, source_target_pairs={{0,1},{1,2},{2,3},{3,4},{4,5},{5,6},{6,7},{7,8},{8,9},{9,10},{10,1... | collective-permute-start | bytes 2457608 | tf_op jit(solution)/shard_map/ppermute | solution.py:233
  43.0 0.7 copy-done.1
  43.7 1.3 collective-permute-start.5
  45.0 0.8 fusion.5
  45.8 0.1 reshape.52
  45.9 0.1 pad.17
  46.1 0.1 reshape.54
  46.2 0.2 slice.192
  46.4 1.7 pad.16
  48.1 1.1 reshape.53
  49.1 1.1 pad_add_fusion
  50.3 1.6 copy.39
  51.8 1.3 collective-permute-start.1
  53.1 4.9 %collective-permute-start = (bf16[4,1056,128]{2,1,0:T(8,128)(2,1)}, bf16[4,1056,128]{2,1,0:T(8,128)(2,1)S(1)}, u32[]{:S(2)}, u32[]{:S(2)}) collective-permute-start(bf16[4,1056,128]{2,1,0:T(8,128)(2,1)} %pad_maximum_fusion), channel_id=1, source_target_pairs={{0,1},{1,2},{2,3},{3,4},{4,5},{5,6},{6,7},{7,8},{8,9},{9,10},{10,1... | collective-permute-start | bytes 3244040 | tf_op jit(solution)/shard_map/ppermute | solution.py:233
  58.1 4.0 %copy-done = bf16[16,2560,128]{2,1,0:T(8,128)(2,1)S(1)} copy-done((bf16[16,2560,128]{2,1,0:T(8,128)(2,1)S(1)}, bf16[16,2560,128]{2,1,0:T(8,128)(2,1)}, u32[]{:S(2)}) %copy-start) | copy-done | bytes 10485784
  62.1 1.0 copy-done.2
  63.0 0.7 copy-done.7
  63.7 0.7 copy-done.14
  64.4 15.1 %fine0.1 = (bf16[16,2560,128]{2,1,0:T(8,128)(2,1)}, bf16[4,64,128]{2,1,0:T(8,128)(2,1)S(1)}) custom-call(bf16[16,2560,128]{2,1,0:T(8,128)(2,1)S(1)} %copy-done, bf16[16,2560,128]{2,1,0:T(8,128)(2,1)S(1)} %copy-done, bf16[16,2560,128]{2,1,0:T(8,128)(2,1)S(1)} %copy-done, bf16[4,288,128]{2,1,0:T(8,128)(2,1)S(1)} %copy-done.2, ...), custom_call_target="tpu_custom_call" | custom-call | flops 2013265920 | bytes 3932160 | tf_op jit(solution)/shard_map/fine0/pallas_call | solution.py:174
  79.5 0.6 copy-done.9
  80.1 28.6 %fine1.1 = (bf16[16,2560,128]{2,1,0:T(8,128)(2,1)}, bf16[4,128,128]{2,1,0:T(8,128)(2,1)}) custom-call(bf16[16,2560,128]{2,1,0:T(8,128)(2,1)S(1)} %copy-done, bf16[16,2560,128]{2,1,0:T(8,128)(2,1)S(1)} %copy-done, bf16[16,2560,128]{2,1,0:T(8,128)(2,1)S(1)} %copy-done, ...), custom_call_target="tpu_custom_call", output_to_operand_aliasing={{0}: (17, {})} | custom-call | flops 4026531840 | bytes 7864320 | tf_op jit(solution)/shard_map/fine1/pallas_call | solution.py:174
  108.7 1.5 collective-permute-start.15
  110.2 41.7 %fine2.1 = (bf16[16,2560,128]{2,1,0:T(8,128)(2,1)}, bf16[4,192,128]{2,1,0:T(8,128)(2,1)S(1)}) custom-call(bf16[16,2560,128]{2,1,0:T(8,128)(2,1)S(1)} %copy-done, bf16[16,2560,128]{2,1,0:T(8,128)(2,1)S(1)} %copy-done, bf16[16,2560,128]{2,1,0:T(8,128)(2,1)S(1)} %copy-done, ...), custom_call_target="tpu_custom_call", output_to_operand_aliasing={{0}: (17, {})} | custom-call | flops 6039797760 | bytes 11796480 | tf_op jit(solution)/shard_map/fine2/pallas_call | solution.py:174
  151.9 55.3 %fine3.1 = (bf16[16,2560,128]{2,1,0:T(8,128)(2,1)}, bf16[4,256,128]{2,1,0:T(8,128)(2,1)S(1)}) custom-call(bf16[16,2560,128]{2,1,0:T(8,128)(2,1)} %refs_2_.7, bf16[16,2560,128]{2,1,0:T(8,128)(2,1)} %refs_2_.7, bf16[16,2560,128]{2,1,0:T(8,128)(2,1)} %refs_2_.7, ...), custom_call_target="tpu_custom_call", output_to_operand_aliasing={{0}: (17, {})} | custom-call | flops 8053063680 | bytes 15728640 | tf_op jit(solution)/shard_map/fine3/pallas_call | solution.py:174
  207.2 1.4 collective-permute-start.17
  208.7 0.2 copy.43
  208.9 0.2 copy.46
  209.1 0.2 copy.47
  209.3 1.3 collective-permute-start.14
  210.6 1.3 collective-permute-start.16
  211.9 7.0 %collective-permute-start.13 = (bf16[4,256,128]{2,1,0:T(8,128)(2,1)S(1)}, bf16[4,256,128]{2,1,0:T(8,128)(2,1)S(1)}, u32[]{:S(2)}, u32[]{:S(2)}) collective-permute-start(bf16[4,256,128]{2,1,0:T(8,128)(2,1)S(1)} %get-tuple-element.20), channel_id=1, source_target_pairs={{0,1},{1,2},{2,3},{3,4},{4,5},{5,6},{6,7},{7,8},{8,9},{9,10},{10,1... | collective-permute-start | bytes 786440 | tf_op jit(solution)/shard_map/ppermute | solution.py:244
  218.9 4.5 %collective-permute-start.11 = (bf16[4,128,128]{2,1,0:T(8,128)(2,1)}, bf16[4,128,128]{2,1,0:T(8,128)(2,1)S(1)}, u32[]{:S(2)}, u32[]{:S(2)}) collective-permute-start(bf16[4,128,128]{2,1,0:T(8,128)(2,1)} %get-tuple-element.18), channel_id=1, source_target_pairs={{0,1},{1,2},{2,3},{3,4},{4,5},{5,6},{6,7},{7,8},{8,9},{9,10},{10,1... | collective-permute-start | bytes 393224 | tf_op jit(solution)/shard_map/ppermute | solution.py:244
  223.5 4.6 %collective-permute-start.12 = (bf16[4,192,128]{2,1,0:T(8,128)(2,1)S(1)}, bf16[4,192,128]{2,1,0:T(8,128)(2,1)S(1)}, u32[]{:S(2)}, u32[]{:S(2)}) collective-permute-start(bf16[4,192,128]{2,1,0:T(8,128)(2,1)S(1)} %copy-done.6), channel_id=1, source_target_pairs={{0,1},{1,2},{2,3},{3,4},{4,5},{5,6},{6,7},{7,8},{8,9},{9,10},{10,1... | collective-permute-start | bytes 589832 | tf_op jit(solution)/shard_map/ppermute | solution.py:244
  228.1 1.0 pad_maximum_fusion.4.refs_0_.refs_1_.refs_2_
  229.1 4.7 %collective-permute-start.10 = (bf16[4,64,128]{2,1,0:T(8,128)(2,1)S(1)}, bf16[4,64,128]{2,1,0:T(8,128)(2,1)S(1)}, u32[]{:S(2)}, u32[]{:S(2)}) collective-permute-start(bf16[4,64,128]{2,1,0:T(8,128)(2,1)S(1)} %copy-done.10), channel_id=1, source_target_pairs={{0,1},{1,2},{2,3},{3,4},{4,5},{5,6},{6,7},{7,8},{8,9},{9,10},{10,1... | collective-permute-start | bytes 196616 | tf_op jit(solution)/shard_map/ppermute | solution.py:244
  233.8 1.0 pad_maximum_fusion.6.refs_6_.refs_7_.refs_8_
  234.8 14.6 %coarse.1 = (bf16[4,640,128]{2,1,0:T(8,128)(2,1)}, f32[8,128]{1,0:T(8,128)S(1)}) custom-call(bf16[4,640,128]{2,1,0:T(8,128)(2,1)S(1)} %pad_maximum_fusion.4.refs_0_.refs_1_.refs_2_, bf16[4,640,128]{2,1,0:T(8,128)(2,1)S(1)} %pad_maximum_fusion.4.refs_0_.refs_1_.refs_2_, bf16[4,640,128]{2,1,0:T(8,128)(2,1)S(1)} %pad_maximum_fusion.4.refs_0_.refs_1_.refs_2_, ...), custom_call_target="tpu_custom_call" | custom-call | flops 2516582400 | bytes 4915200 | tf_op jit(solution)/shard_map/coarse/pallas_call | solution.py:174
  249.4 32.4 %all-reduce.4 = (f32[128]{0:T(128)S(1)}, f32[]{:T(128)}) all-reduce(f32[128]{0:T(128)S(1)} %reduce_sum.18, f32[]{:T(128)} %convert_reduce_fusion), channel_id=1, replica_groups=mesh['parts'=2,'tile'=16] {'tile'}, use_global_device_ids=true, to_apply=%region_1.2 | all-reduce | flops 129 | bytes 1032 | tf_op jit(solution)/shard_map/psum | solution.py:253
  281.8 1.2 broadcast_divide_fusion
  (70 shorter events, 0.4 us)
Async XLA Ops:
  0.6 17.5 %copy-start.19 = (bf16[5,128,128]{2,1,0:T(8,128)(2,1)S(1)}, bf16[5,128,128]{2,1,0:T(8,128)(2,1)}, u32[]{:S(2)}) copy-start(bf16[5,128,128]{2,1,0:T(8,128)(2,1)} %param.23) | copy-start | bytes 491524
  0.6 30.5 %collective-permute-start.18 = (s32[4,640]{1,0:T(4,128)}, s32[4,640]{1,0:T(4,128)S(1)}, u32[]{:S(2)}, u32[]{:S(2)}) collective-permute-start(s32[4,640]{1,0:T(4,128)} %param.22), channel_id=1, source_target_pairs={{0,1},{1,2},{2,3},{3,4},{4,5},{5,6},{6,7},{7,8},{8,9},{9,10},{10,1... | collective-permute-start | bytes 30728 | tf_op jit(solution)/shard_map/ppermute | solution.py:200
  3.1 29.2 %collective-permute-start.19 = (s32[4,640]{1,0:T(4,128)}, s32[4,640]{1,0:T(4,128)S(1)}, u32[]{:S(2)}, u32[]{:S(2)}) collective-permute-start(s32[4,640]{1,0:T(4,128)} %param.22), channel_id=1, source_target_pairs={{1,0},{2,1},{3,2},{4,3},{5,4},{6,5},{7,6},{8,7},{9,8},{10,9},{11,1... | collective-permute-start | bytes 30728 | tf_op jit(solution)/shard_map/ppermute | solution.py:201
  5.4 32.7 %collective-permute-start.2 = (s32[4,2560]{1,0:T(4,128)S(1)}, s32[4,2560]{1,0:T(4,128)S(1)}, u32[]{:S(2)}, u32[]{:S(2)}) collective-permute-start(s32[4,2560]{1,0:T(4,128)S(1)} %get-tuple-element.49), channel_id=1, source_target_pairs={{0,1},{1,2},{2,3},{3,4},{4,5},{5,6},{6,7},{7,8},{8,9},{9,10},{10,1... | collective-permute-start | bytes 122888 | tf_op jit(solution)/shard_map/ppermute | solution.py:200
  10.6 28.8 %collective-permute-start.3 = (s32[4,2560]{1,0:T(4,128)S(1)}, s32[4,2560]{1,0:T(4,128)S(1)}, u32[]{:S(2)}, u32[]{:S(2)}) collective-permute-start(s32[4,2560]{1,0:T(4,128)S(1)} %get-tuple-element.50), channel_id=1, source_target_pairs={{1,0},{2,1},{3,2},{4,3},{5,4},{6,5},{7,6},{8,7},{9,8},{10,9},{11,1... | collective-permute-start | bytes 122888 | tf_op jit(solution)/shard_map/ppermute | solution.py:201
  13.9 29.1 %collective-permute-start.8 = (bf16[4,288,128]{2,1,0:T(8,128)(2,1)S(1)}, bf16[4,288,128]{2,1,0:T(8,128)(2,1)S(1)}, u32[]{:S(2)}, u32[]{:S(2)}) collective-permute-start(bf16[4,288,128]{2,1,0:T(8,128)(2,1)S(1)} %pad_maximum_fusion.9), channel_id=1, source_target_pairs={{0,1},{1,2},{2,3},{3,4},{4,5},{5,6},{6,7},{7,8},{8,9},{9,10},{10,1... | collective-permute-start | bytes 884744 | tf_op jit(solution)/shard_map/ppermute | solution.py:233
  21.0 1.8 copy-start.20
  29.4 1.1 copy-start.21
  29.4 13.5 %copy-start.18 = (s32[16,2560]{1,0:T(8,128)S(1)}, s32[16,2560]{1,0:T(8,128)}, u32[]{:S(2)}) copy-start(s32[16,2560]{1,0:T(8,128)} %param.21) | copy-start | bytes 491524
  31.1 20.7 %collective-permute-start.9 = (bf16[4,288,128]{2,1,0:T(8,128)(2,1)}, bf16[4,288,128]{2,1,0:T(8,128)(2,1)}, u32[]{:S(2)}, u32[]{:S(2)}) collective-permute-start(bf16[4,288,128]{2,1,0:T(8,128)(2,1)} %pad_maximum_fusion.10), channel_id=1, source_target_pairs={{1,0},{2,1},{3,2},{4,3},{5,4},{6,5},{7,6},{8,7},{9,8},{10,9},{11,1... | collective-permute-start | bytes 884744 | tf_op jit(solution)/shard_map/ppermute | solution.py:234
  32.4 20.7 %collective-permute-start.6 = (bf16[4,544,128]{2,1,0:T(8,128)(2,1)}, bf16[4,544,128]{2,1,0:T(8,128)(2,1)}, u32[]{:S(2)}, u32[]{:S(2)}) collective-permute-start(bf16[4,544,128]{2,1,0:T(8,128)(2,1)} %pad_maximum_fusion.7), channel_id=1, source_target_pairs={{0,1},{1,2},{2,3},{3,4},{4,5},{5,6},{6,7},{7,8},{8,9},{9,10},{10,1... | collective-permute-start | bytes 1671176 | tf_op jit(solution)/shard_map/ppermute | solution.py:233
  38.1 42.0 %collective-permute-start.7 = (bf16[4,544,128]{2,1,0:T(8,128)(2,1)}, bf16[4,544,128]{2,1,0:T(8,128)(2,1)}, u32[]{:S(2)}, u32[]{:S(2)}) collective-permute-start(bf16[4,544,128]{2,1,0:T(8,128)(2,1)} %pad_maximum_fusion.8), channel_id=1, source_target_pairs={{1,0},{2,1},{3,2},{4,3},{5,4},{6,5},{7,6},{8,7},{9,8},{10,9},{11,1... | collective-permute-start | bytes 1671176 | tf_op jit(solution)/shard_map/ppermute | solution.py:234
  39.4 70.8 %collective-permute-start.4 = (bf16[4,800,128]{2,1,0:T(8,128)(2,1)}, bf16[4,800,128]{2,1,0:T(8,128)(2,1)S(1)}, u32[]{:S(2)}, u32[]{:S(2)}) collective-permute-start(bf16[4,800,128]{2,1,0:T(8,128)(2,1)} %pad_maximum_fusion.2), channel_id=1, source_target_pairs={{0,1},{1,2},{2,3},{3,4},{4,5},{5,6},{6,7},{7,8},{8,9},{9,10},{10,1... | collective-permute-start | bytes 2457608 | tf_op jit(solution)/shard_map/ppermute | solution.py:233
  43.0 0.7 copy-start.1
  43.7 66.5 %collective-permute-start.5 = (bf16[4,800,128]{2,1,0:T(8,128)(2,1)}, bf16[4,800,128]{2,1,0:T(8,128)(2,1)S(1)}, u32[]{:S(2)}, u32[]{:S(2)}) collective-permute-start(bf16[4,800,128]{2,1,0:T(8,128)(2,1)} %pad_maximum_fusion.3), channel_id=1, source_target_pairs={{1,0},{2,1},{3,2},{4,3},{5,4},{6,5},{7,6},{8,7},{9,8},{10,9},{11,1... | collective-permute-start | bytes 2457608 | tf_op jit(solution)/shard_map/ppermute | solution.py:234
  50.3 7.8 %copy-start.3 = (s32[80,256]{1,0:T(8,128)S(1)}, s32[80,256]{1,0:T(8,128)}, u32[]{:S(2)}) copy-start(s32[80,256]{1,0:T(8,128)} %constant.14.clone.refs_10_) | copy-start | bytes 245764
  50.3 7.8 %copy-start.4 = (bf16[64,256]{1,0:T(8,128)(2,1)S(1)}, bf16[64,256]{1,0:T(8,128)(2,1)}, u32[]{:S(2)}) copy-start(bf16[64,256]{1,0:T(8,128)(2,1)} %constant.15.clone.refs_15_) | copy-start | bytes 98308
  51.8 100.0 %collective-permute-start.1 = (bf16[4,1056,128]{2,1,0:T(8,128)(2,1)}, bf16[4,1056,128]{2,1,0:T(8,128)(2,1)S(1)}, u32[]{:S(2)}, u32[]{:S(2)}) collective-permute-start(bf16[4,1056,128]{2,1,0:T(8,128)(2,1)} %pad_maximum_fusion.1), channel_id=1, source_target_pairs={{1,0},{2,1},{3,2},{4,3},{5,4},{6,5},{7,6},{8,7},{9,8},{10,9},{11,1... | collective-permute-start | bytes 3244040 | tf_op jit(solution)/shard_map/ppermute | solution.py:234
  53.1 98.7 %collective-permute-start = (bf16[4,1056,128]{2,1,0:T(8,128)(2,1)}, bf16[4,1056,128]{2,1,0:T(8,128)(2,1)S(1)}, u32[]{:S(2)}, u32[]{:S(2)}) collective-permute-start(bf16[4,1056,128]{2,1,0:T(8,128)(2,1)} %pad_maximum_fusion), channel_id=1, source_target_pairs={{0,1},{1,2},{2,3},{3,4},{4,5},{5,6},{6,7},{7,8},{8,9},{9,10},{10,1... | collective-permute-start | bytes 3244040 | tf_op jit(solution)/shard_map/ppermute | solution.py:233
  58.1 4.0 %copy-start = (bf16[16,2560,128]{2,1,0:T(8,128)(2,1)S(1)}, bf16[16,2560,128]{2,1,0:T(8,128)(2,1)}, u32[]{:S(2)}) copy-start(bf16[16,2560,128]{2,1,0:T(8,128)(2,1)} %refs_2_.7) | copy-start | bytes 31457284
  62.1 1.0 copy-start.2
  63.0 0.7 copy-start.7
  63.7 0.7 copy-start.14
  64.4 15.7 %copy-start.8 = (bf16[16,64]{1,0:T(8,128)(2,1)S(1)}, bf16[16,64]{1,0:T(8,128)(2,1)}, u32[]{:S(2)}) copy-start(bf16[16,64]{1,0:T(8,128)(2,1)} %constant.16.clone.refs_16_) | copy-start | bytes 6148
  64.4 15.7 %copy-start.15 = (f32[128]{0:T(128)S(1)}, f32[128]{0:T(128)}, u32[]{:S(2)}) copy-start(f32[128]{0:T(128)} %param.24) | copy-start | bytes 1540
  79.5 0.6 copy-start.9
  108.7 114.8 %collective-permute-start.15 = (bf16[4,128,128]{2,1,0:T(8,128)(2,1)}, bf16[4,128,128]{2,1,0:T(8,128)(2,1)}, u32[]{:S(2)}, u32[]{:S(2)}) collective-permute-start(bf16[4,128,128]{2,1,0:T(8,128)(2,1)} %get-tuple-element.18), channel_id=1, source_target_pairs={{1,0},{2,1},{3,2},{4,3},{5,4},{6,5},{7,6},{8,7},{9,8},{10,9},{11,1... | collective-permute-start | bytes 393224 | tf_op jit(solution)/shard_map/ppermute | solution.py:245
  151.9 55.3 %copy-start.5 = (bf16[4,192,128]{2,1,0:T(8,128)(2,1)}, bf16[4,192,128]{2,1,0:T(8,128)(2,1)S(1)}, u32[]{:S(2)}) copy-start(bf16[4,192,128]{2,1,0:T(8,128)(2,1)S(1)} %get-tuple-element.19) | copy-start | bytes 589828
  151.9 56.7 %copy-start.17 = (s32[12,640]{1,0:T(8,128)S(1)}, s32[12,640]{1,0:T(8,128)}, u32[]{:S(2)}) copy-start(s32[12,640]{1,0:T(8,128)} %pad_add_fusion.2) | copy-start | bytes 92164
  207.2 2.1 copy-start.10
  207.2 3.4 %copy-start.6 = (bf16[4,192,128]{2,1,0:T(8,128)(2,1)S(1)}, bf16[4,192,128]{2,1,0:T(8,128)(2,1)}, u32[]{:S(2)}) copy-start(bf16[4,192,128]{2,1,0:T(8,128)(2,1)} %copy-done.5) | copy-start | bytes 589828
  207.2 26.6 %collective-permute-start.17 = (bf16[4,256,128]{2,1,0:T(8,128)(2,1)S(1)}, bf16[4,256,128]{2,1,0:T(8,128)(2,1)S(1)}, u32[]{:S(2)}, u32[]{:S(2)}) collective-permute-start(bf16[4,256,128]{2,1,0:T(8,128)(2,1)S(1)} %get-tuple-element.20), channel_id=1, source_target_pairs={{1,0},{2,1},{3,2},{4,3},{5,4},{6,5},{7,6},{8,7},{9,8},{10,9},{11,1... | collective-permute-start | bytes 786440 | tf_op jit(solution)/shard_map/ppermute | solution.py:245
  209.3 9.6 %collective-permute-start.14 = (bf16[4,64,128]{2,1,0:T(8,128)(2,1)S(1)}, bf16[4,64,128]{2,1,0:T(8,128)(2,1)S(1)}, u32[]{:S(2)}, u32[]{:S(2)}) collective-permute-start(bf16[4,64,128]{2,1,0:T(8,128)(2,1)S(1)} %copy-done.10), channel_id=1, source_target_pairs={{1,0},{2,1},{3,2},{4,3},{5,4},{6,5},{7,6},{8,7},{9,8},{10,9},{11,1... | collective-permute-start | bytes 196616 | tf_op jit(solution)/shard_map/ppermute | solution.py:245
  210.6 18.4 %collective-permute-start.16 = (bf16[4,192,128]{2,1,0:T(8,128)(2,1)S(1)}, bf16[4,192,128]{2,1,0:T(8,128)(2,1)S(1)}, u32[]{:S(2)}, u32[]{:S(2)}) collective-permute-start(bf16[4,192,128]{2,1,0:T(8,128)(2,1)S(1)} %copy-done.6), channel_id=1, source_target_pairs={{1,0},{2,1},{3,2},{4,3},{5,4},{6,5},{7,6},{8,7},{9,8},{10,9},{11,1... | collective-permute-start | bytes 589832 | tf_op jit(solution)/shard_map/ppermute | solution.py:245
  211.9 22.8 %collective-permute-start.13 = (bf16[4,256,128]{2,1,0:T(8,128)(2,1)S(1)}, bf16[4,256,128]{2,1,0:T(8,128)(2,1)S(1)}, u32[]{:S(2)}, u32[]{:S(2)}) collective-permute-start(bf16[4,256,128]{2,1,0:T(8,128)(2,1)S(1)} %get-tuple-element.20), channel_id=1, source_target_pairs={{0,1},{1,2},{2,3},{3,4},{4,5},{5,6},{6,7},{7,8},{8,9},{9,10},{10,1... | collective-permute-start | bytes 786440 | tf_op jit(solution)/shard_map/ppermute | solution.py:244
  218.9 15.8 %collective-permute-start.11 = (bf16[4,128,128]{2,1,0:T(8,128)(2,1)}, bf16[4,128,128]{2,1,0:T(8,128)(2,1)S(1)}, u32[]{:S(2)}, u32[]{:S(2)}) collective-permute-start(bf16[4,128,128]{2,1,0:T(8,128)(2,1)} %get-tuple-element.18), channel_id=1, source_target_pairs={{0,1},{1,2},{2,3},{3,4},{4,5},{5,6},{6,7},{7,8},{8,9},{9,10},{10,1... | collective-permute-start | bytes 393224 | tf_op jit(solution)/shard_map/ppermute | solution.py:244
  223.5 11.2 %collective-permute-start.12 = (bf16[4,192,128]{2,1,0:T(8,128)(2,1)S(1)}, bf16[4,192,128]{2,1,0:T(8,128)(2,1)S(1)}, u32[]{:S(2)}, u32[]{:S(2)}) collective-permute-start(bf16[4,192,128]{2,1,0:T(8,128)(2,1)S(1)} %copy-done.6), channel_id=1, source_target_pairs={{0,1},{1,2},{2,3},{3,4},{4,5},{5,6},{6,7},{7,8},{8,9},{9,10},{10,1... | collective-permute-start | bytes 589832 | tf_op jit(solution)/shard_map/ppermute | solution.py:244
  229.0 5.8 %copy-start.11 = (bf16[2,128,128]{2,1,0:T(8,128)(2,1)S(1)}, bf16[2,128,128]{2,1,0:T(8,128)(2,1)}, u32[]{:S(2)}) copy-start(bf16[2,128,128]{2,1,0:T(8,128)(2,1)} %get-tuple-element.45) | copy-start | bytes 196612
  229.0 5.8 %copy-start.12 = (bf16[2,128,128]{2,1,0:T(8,128)(2,1)S(1)}, bf16[2,128,128]{2,1,0:T(8,128)(2,1)}, u32[]{:S(2)}) copy-start(bf16[2,128,128]{2,1,0:T(8,128)(2,1)} %get-tuple-element.46) | copy-start | bytes 196612
  229.0 5.8 %copy-start.13 = (bf16[128,128]{1,0:T(8,128)(2,1)S(1)}, bf16[128,128]{1,0:T(8,128)(2,1)}, u32[]{:S(2)}) copy-start(bf16[128,128]{1,0:T(8,128)(2,1)} %slice_bitcast_fusion.refs_13_) | copy-start | bytes 98308
  229.0 5.8 %copy-start.16 = (f32[128]{0:T(128)S(1)}, f32[128]{0:T(128)}, u32[]{:S(2)}) copy-start(f32[128]{0:T(128)} %param.26) | copy-start | bytes 1540
  229.1 5.6 %collective-permute-start.10 = (bf16[4,64,128]{2,1,0:T(8,128)(2,1)S(1)}, bf16[4,64,128]{2,1,0:T(8,128)(2,1)S(1)}, u32[]{:S(2)}, u32[]{:S(2)}) collective-permute-start(bf16[4,64,128]{2,1,0:T(8,128)(2,1)S(1)} %copy-done.10), channel_id=1, source_target_pairs={{0,1},{1,2},{2,3},{3,4},{4,5},{5,6},{6,7},{7,8},{8,9},{9,10},{10,1... | collective-permute-start | bytes 196616 | tf_op jit(solution)/shard_map/ppermute | solution.py:244

commit v2 on v1

--- a/solution.py
+++ b/solution.py
@@ -37,8 +37,8 @@
 
 
 def window_kernel(rows, pool, refs):
-    (main, left, right, tmain, tleft, tright, bmain, bleft, bright, codes, bits, w01, w23, w4, bias) = refs[:15]
-    rest = refs[15:]
+    (main, left, right, tmain, tleft, tright, bmain, bleft, bright, codes, outer, bits, w01, w23, w4, bias) = refs[:16]
+    rest = refs[16:]
     if pool:
         pool1, pool2, _, out, coarse = rest[:5]
         rest = rest[5:]
@@ -56,12 +56,21 @@
         if not pool:
             sums[...] = jnp.zeros_like(sums)
 
-    code = codes[0]
-    degree = jnp.zeros(code.shape, jnp.int32)
-    for bit in range(8):
-        degree = degree + ((code >> bit) & 1)
-    scale = -2.0 / jnp.maximum(degree.astype(jnp.float32), 1.0)
-    real = ((code >> 8) & 1).astype(jnp.float32)
+    def tables(code):
+        degree = jnp.zeros(code.shape, jnp.int32)
+        for bit in range(8):
+            degree = degree + ((code >> bit) & 1)
+        return code, -2.0 / jnp.maximum(degree.astype(jnp.float32), 1.0), ((code >> 8) & 1).astype(jnp.float32)
+
+    inside, beyond = tables(codes[0]), tables(outer[0])
+
+    def column(which, r):
+        if r < DEEP:
+            return beyond[which][:, r : r + 1]
+        if r < DEEP + rows:
+            return inside[which][:, r - DEEP : r - DEEP + 1]
+        return beyond[which][:, r - rows : r - rows + 1]
+
     table = bits[...]
     low = lax.broadcasted_iota(jnp.int32, (EDGE, 128), 0) < 8
 
@@ -72,14 +81,14 @@
             m, a, b, s = main, left, right, r - DEEP
         else:
             m, a, b, s = bmain, bleft, bright, r - DEEP - rows
-        mask = jnp.broadcast_to(real[:, r : r + 1], (WIN, 128))
+        mask = jnp.broadcast_to(column(2, r), (WIN, 128))
         side = jnp.where(low, b[s].astype(jnp.float32), a[s].astype(jnp.float32))
         p0[pl.ds(r * WIN, USE), :] = (m[s].astype(jnp.float32) * mask[:USE]).astype(jnp.bfloat16)
         p0[pl.ds(r * WIN + USE, EDGE), :] = (side * mask[USE:]).astype(jnp.bfloat16)
         if 1 <= r < full - 1:
-            wide = jnp.broadcast_to(code[:, r : r + 1], (WIN, 256))
+            wide = jnp.broadcast_to(column(0, r), (WIN, 256))
             links[r] = jnp.where((wide & table) != 0, 1.0, 0.0).astype(jnp.bfloat16)
-            coef[r] = jnp.broadcast_to(scale[:, r : r + 1], (WIN, 128))
+            coef[r] = jnp.broadcast_to(column(1, r), (WIN, 128))
 
     terms = (p0, p1, p2, p3, p4)
     for k in range(1, 5):
@@ -103,7 +112,7 @@
         mixed += jnp.dot(jnp.concatenate([q[2], q[3]], axis=1), w23[...], preferred_element_type=jnp.float32)
         mixed += jnp.dot(q[4], w4[...], preferred_element_type=jnp.float32)
         mask = jnp.concatenate(
-            [jnp.broadcast_to(real[:USE, first + j : first + j + 1], (USE, 128)) for j in range(group)], axis=0
+            [jnp.broadcast_to(column(2, first + j)[:USE], (USE, 128)) for j in range(group)], axis=0
         )
         res = (mask * jnp.maximum(mixed + bias[...], 0.0)).astype(jnp.bfloat16)
         for j in range(group):
@@ -115,10 +124,10 @@
             sums[...] += jnp.sum(res.astype(jnp.float32).reshape(-1, 8, 128), axis=0)
 
 
-def layer(name, main, top, bottom, codes, weights, bias, first, count, pool, canvas=None):
+def layer(name, main, top, bottom, origin, codes, outer, weights, bias, first, count, pool, canvas=None):
     rows, cols, width = main.shape
     total = cols // USE
-    chunked = top.shape[1] != cols
+    held = top.shape[1] // EDGE
     ratio = USE // EDGE
 
     def spec(n, pick, size):
@@ -130,14 +139,11 @@
     def right_of(w):
         return jnp.minimum((first + w) * ratio + ratio, total * ratio - 1)
 
-    if chunked:
-        halo = [
-            spec(DEEP, lambda w: w, USE),
-            spec(DEEP, lambda w: jnp.where(w == 0, count * ratio + 1, w * ratio - 1), EDGE),
-            spec(DEEP, lambda w: w * ratio + ratio, EDGE),
-        ]
-    else:
-        halo = [spec(DEEP, lambda w: first + w, USE), spec(DEEP, left_of, EDGE), spec(DEEP, right_of, EDGE)]
+    halo = [
+        spec(DEEP, lambda w: first + w - origin, USE),
+        spec(DEEP, lambda w: jnp.maximum((first + w - origin) * ratio - 1, 0), EDGE),
+        spec(DEEP, lambda w: jnp.minimum((first + w - origin) * ratio + ratio, held - 1), EDGE),
+    ]
 
     def whole(*shape):
         return pl.BlockSpec(shape, lambda w: (0,) * len(shape))
@@ -146,10 +152,11 @@
     in_specs = (
         [spec(rows, lambda w: first + w, USE), spec(rows, left_of, EDGE), spec(rows, right_of, EDGE)]
         + halo + halo
-        + [pl.BlockSpec((1, WIN, full), lambda w: (first + w, 0, 0))]
+        + [pl.BlockSpec((1, WIN, rows), lambda w: (first + w, 0, 0))]
+        + [pl.BlockSpec((1, WIN, 2 * DEEP), lambda w: (first + w, 0, 0))]
         + [whole(WIN, 256), whole(256, 128), whole(256, 128), whole(128, 128), whole(1, 128)]
     )
-    operands = [main] * 3 + [top] * 3 + [bottom] * 3 + [codes, jnp.asarray(bit_table())]
+    operands = [main] * 3 + [top] * 3 + [bottom] * 3 + [codes, outer, jnp.asarray(bit_table())]
     operands += [weights[0:2].reshape(256, 128), weights[2:4].reshape(256, 128), weights[4], bias.reshape(1, 128)]
     out_map = jax.ShapeDtypeStruct((rows, cols, width), jnp.bfloat16)
     aliases = {}
@@ -195,11 +202,7 @@
     return up, down
 
 
-def code_windows(links):
-    up, down = shifts()
-    above = lax.ppermute(links[-DEEP:], "tile", up)
-    below = lax.ppermute(links[:DEEP], "tile", down)
-    codes = jnp.concatenate([above, links, below], axis=0)
+def code_windows(codes):
     rows, cols = codes.shape
     count = cols // USE
     body = codes.reshape(rows, count, USE)
@@ -208,50 +211,124 @@
     return jnp.concatenate([body, after, before], axis=2).transpose(1, 2, 0)
 
 
-CHUNKS = (0.1, 0.3, 0.6, 1.0)
+def coded(codes):
+    return jnp.stack([codes & 255, codes >> 8]).astype(jnp.bfloat16).reshape(-1, 128)
+
+
+def decoded(lines, shape):
+    pair = lines.reshape((2,) + shape).astype(jnp.int32)
+    return pair[0] + 256 * pair[1]
+
+
+def total_kernel(size, part, pooled, slots, send_sem, recv_sem):
+    me = lax.axis_index("tile")
+    barrier = pltpu.get_barrier_semaphore()
+    for hop in range(1, size):
+        pl.semaphore_signal(
+            barrier, inc=1, device_id={"tile": lax.rem(me + hop, size)}, device_id_type=pl.DeviceIdType.MESH
+        )
+    pl.semaphore_wait(barrier, size - 1)
+
+    def copy(hop):
+        return pltpu.make_async_remote_copy(
+            src_ref=part,
+            dst_ref=slots.at[me],
+            send_sem=send_sem.at[hop],
+            recv_sem=recv_sem.at[hop],
+            device_id={"tile": lax.rem(me + hop, size)},
+            device_id_type=pl.DeviceIdType.MESH,
+        )
+
+    copies = [copy(hop) for hop in range(1, size)]
+    for one in copies:
+        one.start()
+    slots[me] = part[...]
+    for hop in range(1, size):
+        sender = lax.rem(me + size - hop, size)
+        pltpu.make_async_remote_copy(
+            src_ref=part,
+            dst_ref=slots.at[sender],
+            send_sem=send_sem.at[hop],
+            recv_sem=recv_sem.at[hop],
+            device_id={"tile": lax.rem(me + hop, size)},
+            device_id_type=pl.DeviceIdType.MESH,
+        ).wait()
+    whole = slots[0]
+    for j in range(1, size):
+        whole = whole + slots[j]
+    pooled[...] = jnp.sum(whole[:8], axis=0, keepdims=True) / whole[8:9]
+
+
+def total_over_tiles(part):
+    size = lax.axis_size("tile")
+    return pl.pallas_call(
+        lambda *refs: total_kernel(size, *refs),
+        in_specs=[pl.BlockSpec(memory_space=pltpu.VMEM)],
+        out_specs=pl.BlockSpec(memory_space=pltpu.VMEM),
+        out_shape=jax.ShapeDtypeStruct((1, 128), jnp.float32),
+        scratch_shapes=[
+            pltpu.VMEM((size, 16, 128), jnp.float32),
+            pltpu.SemaphoreType.DMA((size,)),
+            pltpu.SemaphoreType.DMA((size,)),
+        ],
+        compiler_params=pltpu.CompilerParams(collective_id=0, has_side_effects=True),
+        name="total",
+    )(part)
+
+
+SPLITS = (0.3, 0.9, 1.0)
 
 
 def on_device(features, links, coarse_links, fine_weight, fine_bias, coarse_weight, coarse_bias):
     up, down = shifts()
     rows, cols, width = features.shape
     total = cols // USE
-    ends = [round(total * f) for f in CHUNKS]
+    ends = [round(total * f) for f in SPLITS]
     starts = [0] + ends[:-1]
+    split = ends[0] * USE
+    near = (DEEP, split + USE, width)
+    lines = near[0] * near[1]
+    fine_lines = DEEP * cols * 2 // 128
+
+    def exchanged(pick, coarse_pick):
+        return jnp.concatenate(
+            [features[pick, : split + USE].reshape(-1, 128), coded(links[pick]), coded(coarse_links[coarse_pick])]
+        )
+
+    last, start = slice(rows - DEEP, rows), slice(0, DEEP)
+    coarse_rows = coarse_links.shape[0]
+    above = lax.ppermute(exchanged(last, slice(coarse_rows - DEEP, coarse_rows)), "tile", up)
+    below = lax.ppermute(exchanged(start, start), "tile", down)
+    far_above = lax.ppermute(features[last, split - USE :], "tile", up)
+    far_below = lax.ppermute(features[start, split - USE :], "tile", down)
     fine_codes = code_windows(links)
     coarse_codes = code_windows(coarse_links)
-    halos = []
-    for lo, hi in zip(starts, ends):
-        a, b = lo * USE, hi * USE
-        right = min(b, cols - EDGE)
-        left = max(a - EDGE, 0)
-
-        def piece(part):
-            return jnp.concatenate(
-                [part[:, a:b], part[:, right : right + EDGE], part[:, left : left + EDGE]], axis=1
-            )
-
-        above = lax.ppermute(piece(features[-DEEP:]), "tile", up)
-        below = lax.ppermute(piece(features[:DEEP]), "tile", down)
-        halos.append((above, below))
+    ghosts = [decoded(part[lines : lines + fine_lines], (DEEP, cols)) for part in (above, below)]
+    fine_outer = code_windows(jnp.concatenate(ghosts))
+    ghosts = [decoded(part[lines + fine_lines :], (DEEP, cols // 4)) for part in (above, below)]
+    coarse_outer = code_windows(jnp.concatenate(ghosts))
+    halos = [(above[:lines].reshape(near), below[:lines].reshape(near), 0)]
+    halos += [(far_above, far_below, ends[0] - 1)] * (len(ends) - 1)
     canvas = None
     mids, tops, bottoms = [], [], []
     for n, (lo, hi) in enumerate(zip(starts, ends)):
-        above, below = halos[n]
         canvas, mid = layer(
-            f"fine{n}", features, above, below, fine_codes, fine_weight, fine_bias, lo, hi - lo, True, canvas
+            f"fine{n}", features, *halos[n], fine_codes, fine_outer, fine_weight, fine_bias, lo, hi - lo, True, canvas
         )
         mids.append(mid)
-        tops.append(lax.ppermute(mid, "tile", up))
-        bottoms.append(lax.ppermute(mid, "tile", down))
+        if n == 0:
+            continue
+        send = jnp.concatenate(mids[:2], axis=1) if n == 1 else mid
+        tops.append(lax.ppermute(send, "tile", up))
+        bottoms.append(lax.ppermute(send, "tile", down))
     coarse_in = jnp.concatenate(mids, axis=1)
-    above = jnp.concatenate(tops, axis=1)
-    below = jnp.concatenate(bottoms, axis=1)
     coarse_map, sums = layer(
-        "coarse", coarse_in, above, below, coarse_codes, coarse_weight, coarse_bias, 0, coarse_in.shape[1] // USE, False
+        "coarse", coarse_in, jnp.concatenate(tops, axis=1), jnp.concatenate(bottoms, axis=1), 0,
+        coarse_codes, coarse_outer, coarse_weight, coarse_bias, 0, coarse_in.shape[1] // USE, False,
     )
     real_count = jnp.sum((coarse_links >> 8 & 1).astype(jnp.float32))
-    totals, counted = lax.psum((jnp.sum(sums, axis=0), real_count), "tile")
-    return (canvas, coarse_map, totals / counted)
+    pooled = total_over_tiles(jnp.concatenate([sums, jnp.broadcast_to(real_count, (8, 128))]))
+    return (canvas, coarse_map, pooled[0])
 
 
 def solution(mesh):

time: 284 us -> 268 us (0.944)
  blocking collectives: 32.4 us -> 0 us
  local copies, waits for them, and re-layouts: 22.7 us -> 41.4 us
  starting transfers between devices: 59.4 us -> 44.3 us
  Pallas kernels: 155 us -> 164 us
  other arithmetic: 12 us -> 14.9 us
    psum x1 -> x0, blocking collectives: 32.4 us -> none  [on_device(): totals, counted = lax.psum((jnp.sum(sums, axis=0), real_count), 'tile')]
    ppermute x20 -> x8, starting transfers between devices: 59.4 us -> 44.3 us  [the longest x2 29.4 us: on_device(): tops.append(lax.ppermute(send, 'tile', up))]
    pallas_call x0 -> x1, Pallas kernels: none -> 12.2 us  [total_over_tiles(): pl.pallas_call(lambda *refs: total_kernel(size, *refs), in_specs=[pl.Bloc...]
    add x0 -> x10, local copies, waits for them, and re-layouts: none -> 8.89 us  [decoded(): return pair[0] + 256 * pair[1]]
    unnamed x46 -> x62, local copies, waits for them, and re-layouts: 7.97 us -> 11.8 us
    pallas_call x5 -> x4, Pallas kernels: 155 us -> 152 us  [layer(): pl.pallas_call(lambda *refs: window_kernel(rows, pool, refs), grid=(count...]
    convert_element_type x0 -> x4, other arithmetic: none -> 2.99 us  [decoded(): pair = lines.reshape((2,) + shape).astype(jnp.int32)]
    concatenate x12 -> x5, other arithmetic: 8.12 us -> 5.16 us  [the longest x1 1.46 us: on_device(): coarse_outer = code_windows(jnp.concatenate(ghosts))]
  transfers between devices with their start and end apart: 20 -> 8, of which waited for: 0 -> 0; matrix products, arithmetic and copies ran while one was open for 9% -> 15% of each run, Pallas kernels for 50% -> 21%
where the time goes in v2:
time: 268 us; the launch traced here: 266 us
  Pallas kernels  164 us (61%)
  starting transfers between devices  44.3 us (17%)
  local copies, waits for them, and re-layouts  41.4 us (15%)
  other arithmetic  14.9 us (6%)
    pallas_call x4, Pallas kernels, layer(): pl.pallas_call(lambda *refs: window_kernel(rows, pool, refs), grid=(count...  152 us
    ppermute x2, starting transfers between devices, on_device(): tops.append(lax.ppermute(send, 'tile', up))  29.4 us
    pallas_call x1, Pallas kernels, total_over_tiles(): pl.pallas_call(lambda *refs: total_kernel(size, *refs), in_specs=[pl.Bloc...  12.2 us
    unnamed x62, local copies, waits for them, and re-layouts  11.8 us
    add x10, local copies, waits for them, and re-layouts, decoded(): return pair[0] + 256 * pair[1]  8.89 us
    ppermute x1, starting transfers between devices, on_device(): far_above = lax.ppermute(features[last, split - USE:], 'tile', up)  6.17 us
  transfers between devices with their start and end apart: 8, of which 0 were waited for; matrix products, arithmetic and copies ran while one was open for 15% of the time, Pallas kernels for 21%

profile of v2, /device:TPU:0, one launch (start us, length us, event | category | flops | bytes accessed | tf_op | source)
XLA Modules:
  0.0 266.3 jit_solution(17317497006202054521)
XLA Ops:
  0.6 0.7 fusion.9
  1.4 1.0 fusion.2
  2.5 1.5 fusion.10
  4.0 1.4 pad_maximum_fusion.1
  5.4 3.3 %collective-permute-start.2 = (bf16[3528,128]{1,0:T(8,128)(2,1)}, bf16[3528,128]{1,0:T(8,128)(2,1)}, u32[]{:S(2)}, u32[]{:S(2)}) collective-permute-start(bf16[3528,128]{1,0:T(8,128)(2,1)} %get-tuple-element.39), channel_id=1, source_target_pairs={{0,1},{1,2},{2,3},{3,4},{4,5},{5,6},{6,7},{7,8},{8,9},{9,10},{10,1... | collective-permute-start | bytes 2709512 | tf_op jit(solution)/shard_map/ppermute | solution.py:300
  8.7 1.4 collective-permute-start.3
  10.1 4.3 %fusion.11 = (bf16[4,1856,128]{2,1,0:T(8,128)(2,1)}, bf16[4,1856,128]{2,1,0:T(8,128)(2,1)}) fusion(bf16[16,2560,128]{2,1,0:T(8,128)(2,1)} %refs_2_.5), kind=kLoop, calls=%fused_computation.46 | loop fusion | bytes 7602176 | tf_op jit(solution)/shard_map/slice | solution.py:303
  14.4 1.3 collective-permute-start.1
  15.7 6.2 %collective-permute-start = (bf16[4,1856,128]{2,1,0:T(8,128)(2,1)}, bf16[4,1856,128]{2,1,0:T(8,128)(2,1)}, u32[]{:S(2)}, u32[]{:S(2)}) collective-permute-start(bf16[4,1856,128]{2,1,0:T(8,128)(2,1)} %get-tuple-element.22), channel_id=1, source_target_pairs={{0,1},{1,2},{2,3},{3,4},{4,5},{5,6},{6,7},{7,8},{8,9},{9,10},{10,1... | collective-permute-start | bytes 5701640 | tf_op jit(solution)/shard_map/ppermute | solution.py:302
  21.9 0.6 convert_reduce_fusion
  22.7 0.2 copy.80
  23.9 0.2 pad_add_fusion
  24.1 1.7 copy.71
  25.8 0.8 add_bitcast_fusion.refs_9_
  26.6 0.6 slice_bitcast_fusion.1.refs_14_
  27.2 0.7 fusion.13
  27.9 0.6 slice_bitcast_fusion.refs_14_
  28.5 0.7 fusion.12
  29.2 0.8 slice_convert_fusion.1
  30.0 0.8 slice_convert_fusion
  31.5 0.8 pad_add_fusion.1
  32.3 1.4 copy.72
  33.9 1.3 slice.194
  35.2 1.2 slice.195
  36.5 41.4 %fine0.1 = (bf16[16,2560,128]{2,1,0:T(8,128)(2,1)}, bf16[4,192,128]{2,1,0:T(8,128)(2,1)S(1)}) custom-call(bf16[16,2560,128]{2,1,0:T(8,128)(2,1)} %refs_2_.5, bf16[16,2560,128]{2,1,0:T(8,128)(2,1)} %refs_2_.5, bf16[16,2560,128]{2,1,0:T(8,128)(2,1)} %refs_2_.5, bf16[4,832,128]{2,1,0:T(8,128)(2,1)S(1)} %bitcast.46, bf16[4,832,128]{2,1,0:T(8,128)(2,1)S(1)} %bitcast.47, ...), custom_call_target="tpu_custom_call" | custom-call | flops 6039797760 | bytes 11796480 | tf_op jit(solution)/shard_map/fine0/pallas_call | solution.py:181
  77.9 0.7 constant_dynamic-update-slice_fusion.1
  78.6 0.7 slice_convert_fusion.3
  79.3 0.6 fusion.7
  79.9 0.7 slice_convert_fusion.2
  80.7 81.1 %fine1.1 = (bf16[16,2560,128]{2,1,0:T(8,128)(2,1)}, bf16[4,384,128]{2,1,0:T(8,128)(2,1)S(1)}) custom-call(bf16[16,2560,128]{2,1,0:T(8,128)(2,1)} %refs_2_.5, bf16[16,2560,128]{2,1,0:T(8,128)(2,1)} %refs_2_.5, bf16[16,2560,128]{2,1,0:T(8,128)(2,1)} %refs_2_.5, ...), custom_call_target="tpu_custom_call", output_to_operand_aliasing={{0}: (18, {})} | custom-call | flops 12079595520 | bytes 23592960 | tf_op jit(solution)/shard_map/fine1/pallas_call | solution.py:181
  161.8 0.8 copy-done.2
  162.5 0.8 constant_dynamic-update-slice_fusion
  163.3 1.3 collective-permute-start.6
  164.6 0.6 fusion.6
  165.2 1.3 add.68
  166.5 1.3 add.69
  167.8 25.1 %collective-permute-start.4 = (bf16[4,576,128]{2,1,0:T(8,128)(2,1)}, bf16[4,576,128]{2,1,0:T(8,128)(2,1)}, u32[]{:S(2)}, u32[]{:S(2)}) collective-permute-start(bf16[4,576,128]{2,1,0:T(8,128)(2,1)} %constant_dynamic-update-slice_fusion), channel_id=1, source_target_pairs={{0,1},{1,2},{2,3},{3,4},{4,5},{5,6},{6,7},{7,8},{8,9},{9,10},{10,1... | collective-permute-start | bytes 1769480 | tf_op jit(solution)/shard_map/ppermute | solution.py:322
  192.9 1.5 slice_add_fusion.1
  194.4 1.4 add.65
  195.8 1.4 add.67
  197.2 1.7 copy.76
  198.8 1.6 copy.87
  200.4 1.0 pad.39.clone
  201.4 0.6 slice.206
  202.0 1.6 copy.88
  203.6 1.0 pad.40.clone
  204.6 0.6 slice.207
  205.2 1.7 copy.77
  206.9 1.3 add_bitcast_fusion.1.refs_10_
  208.2 1.4 copy-done.1
  209.6 0.8 copy-done.5
  210.4 0.8 copy-done.7
  211.3 0.9 copy-done.11
  212.2 0.8 copy-done.14
  212.9 0.8 copy-done.17
  213.7 15.1 %fine2.1 = (bf16[16,2560,128]{2,1,0:T(8,128)(2,1)}, bf16[4,64,128]{2,1,0:T(8,128)(2,1)S(1)}) custom-call(bf16[16,2560,128]{2,1,0:T(8,128)(2,1)} %refs_2_.5, bf16[16,2560,128]{2,1,0:T(8,128)(2,1)} %refs_2_.5, bf16[16,2560,128]{2,1,0:T(8,128)(2,1)} %refs_2_.5, ...), custom_call_target="tpu_custom_call", output_to_operand_aliasing={{0}: (18, {})} | custom-call | flops 2013265920 | bytes 3932160 | tf_op jit(solution)/shard_map/fine2/pallas_call | solution.py:181
  228.9 1.4 collective-permute-start.7
  230.3 4.4 %collective-permute-start.5 = (bf16[4,64,128]{2,1,0:T(8,128)(2,1)S(1)}, bf16[4,64,128]{2,1,0:T(8,128)(2,1)S(1)}, u32[]{:S(2)}, u32[]{:S(2)}) collective-permute-start(bf16[4,64,128]{2,1,0:T(8,128)(2,1)S(1)} %get-tuple-element.16), channel_id=1, source_target_pairs={{0,1},{1,2},{2,3},{3,4},{4,5},{5,6},{6,7},{7,8},{8,9},{9,10},{10,1... | collective-permute-start | bytes 196616 | tf_op jit(solution)/shard_map/ppermute | solution.py:322
  234.8 1.1 pad_maximum_fusion.4.refs_6_.refs_7_.refs_8_
  235.9 1.1 pad_maximum_fusion.3.refs_3_.refs_4_.refs_5_
  237.1 14.6 %coarse.1 = (bf16[4,640,128]{2,1,0:T(8,128)(2,1)}, f32[8,128]{1,0:T(8,128)S(1)}) custom-call(bf16[4,640,128]{2,1,0:T(8,128)(2,1)S(1)} %pad_maximum_fusion.2.refs_0_.refs_1_.refs_2_, bf16[4,640,128]{2,1,0:T(8,128)(2,1)S(1)} %pad_maximum_fusion.2.refs_0_.refs_1_.refs_2_, bf16[4,640,128]{2,1,0:T(8,128)(2,1)S(1)} %pad_maximum_fusion.2.refs_0_.refs_1_.refs_2_, ...), custom_call_target="tpu_custom_call" | custom-call | flops 2516582400 | bytes 4915200 | tf_op jit(solution)/shard_map/coarse/pallas_call | solution.py:181
  251.6 1.2 concatenate.59.refs_0_
  252.9 12.2 %total.1 = f32[1,128]{1,0:T(1,128)} custom-call(f32[16,128]{1,0:T(8,128)} %concatenate.59.refs_0_), custom_call_target="tpu_custom_call" | custom-call | tf_op jit(solution)/shard_map/total/pallas_call | solution.py:264
  265.1 1.2 copy.93
  (89 shorter events, 2.1 us)
Async XLA Ops:
  5.4 23.8 %collective-permute-start.2 = (bf16[3528,128]{1,0:T(8,128)(2,1)}, bf16[3528,128]{1,0:T(8,128)(2,1)}, u32[]{:S(2)}, u32[]{:S(2)}) collective-permute-start(bf16[3528,128]{1,0:T(8,128)(2,1)} %get-tuple-element.39), channel_id=1, source_target_pairs={{0,1},{1,2},{2,3},{3,4},{4,5},{5,6},{6,7},{7,8},{8,9},{9,10},{10,1... | collective-permute-start | bytes 2709512 | tf_op jit(solution)/shard_map/ppermute | solution.py:300
  8.7 13.2 %copy-start.25 = (s32[4,640]{1,0:T(4,128)S(1)}, s32[4,640]{1,0:T(4,128)}, u32[]{:S(2)}) copy-start(s32[4,640]{1,0:T(4,128)} %param.19) | copy-start | bytes 30724
  8.7 13.8 %copy-start.24 = (s32[16,2560]{1,0:T(8,128)S(1)}, s32[16,2560]{1,0:T(8,128)}, u32[]{:S(2)}) copy-start(s32[16,2560]{1,0:T(8,128)} %param.18) | copy-start | bytes 491524
  8.7 21.3 %collective-permute-start.3 = (bf16[3528,128]{1,0:T(8,128)(2,1)}, bf16[3528,128]{1,0:T(8,128)(2,1)}, u32[]{:S(2)}, u32[]{:S(2)}) collective-permute-start(bf16[3528,128]{1,0:T(8,128)(2,1)} %get-tuple-element.40), channel_id=1, source_target_pairs={{1,0},{2,1},{3,2},{4,3},{5,4},{6,5},{7,6},{8,7},{9,8},{10,9},{11,1... | collective-permute-start | bytes 2709512 | tf_op jit(solution)/shard_map/ppermute | solution.py:301
  14.4 66.3 %collective-permute-start.1 = (bf16[4,1856,128]{2,1,0:T(8,128)(2,1)}, bf16[4,1856,128]{2,1,0:T(8,128)(2,1)S(1)}, u32[]{:S(2)}, u32[]{:S(2)}) collective-permute-start(bf16[4,1856,128]{2,1,0:T(8,128)(2,1)} %get-tuple-element.21), channel_id=1, source_target_pairs={{1,0},{2,1},{3,2},{4,3},{5,4},{6,5},{7,6},{8,7},{9,8},{10,9},{11,1... | collective-permute-start | bytes 5701640 | tf_op jit(solution)/shard_map/ppermute | solution.py:303
  15.7 65.0 %collective-permute-start = (bf16[4,1856,128]{2,1,0:T(8,128)(2,1)}, bf16[4,1856,128]{2,1,0:T(8,128)(2,1)}, u32[]{:S(2)}, u32[]{:S(2)}) collective-permute-start(bf16[4,1856,128]{2,1,0:T(8,128)(2,1)} %get-tuple-element.22), channel_id=1, source_target_pairs={{0,1},{1,2},{2,3},{3,4},{4,5},{5,6},{6,7},{7,8},{8,9},{9,10},{10,1... | collective-permute-start | bytes 5701640 | tf_op jit(solution)/shard_map/ppermute | solution.py:302
  23.9 2.7 %copy-start.26 = (bf16[5,128,128]{2,1,0:T(8,128)(2,1)S(1)}, bf16[5,128,128]{2,1,0:T(8,128)(2,1)}, u32[]{:S(2)}) copy-start(bf16[5,128,128]{2,1,0:T(8,128)(2,1)} %param.20) | copy-start | bytes 491524
  24.1 3.8 %copy-start.27 = (bf16[5,128,128]{2,1,0:T(8,128)(2,1)S(1)}, bf16[5,128,128]{2,1,0:T(8,128)(2,1)}, u32[]{:S(2)}) copy-start(bf16[5,128,128]{2,1,0:T(8,128)(2,1)} %param.22) | copy-start | bytes 491524
  33.8 2.6 copy-start
  33.8 2.6 copy-start.4
  33.8 2.6 copy-start.6
  33.8 2.6 copy-start.10
  33.8 2.6 copy-start.13
  33.8 2.6 copy-start.16
  33.8 2.6 copy-start.20
  33.8 2.6 copy-start.22
  77.9 2.8 %copy-start.8 = (bf16[4,192,128]{2,1,0:T(8,128)(2,1)}, bf16[4,192,128]{2,1,0:T(8,128)(2,1)S(1)}, u32[]{:S(2)}) copy-start(bf16[4,192,128]{2,1,0:T(8,128)(2,1)S(1)} %get-tuple-element.14) | copy-start | bytes 589828
  161.8 0.8 copy-start.2
  163.3 71.4 %collective-permute-start.6 = (bf16[4,576,128]{2,1,0:T(8,128)(2,1)}, bf16[4,576,128]{2,1,0:T(8,128)(2,1)}, u32[]{:S(2)}, u32[]{:S(2)}) collective-permute-start(bf16[4,576,128]{2,1,0:T(8,128)(2,1)} %constant_dynamic-update-slice_fusion), channel_id=1, source_target_pairs={{1,0},{2,1},{3,2},{4,3},{5,4},{6,5},{7,6},{8,7},{9,8},{10,9},{11,1... | collective-permute-start | bytes 1769480 | tf_op jit(solution)/shard_map/ppermute | solution.py:323
  167.8 68.1 %collective-permute-start.4 = (bf16[4,576,128]{2,1,0:T(8,128)(2,1)}, bf16[4,576,128]{2,1,0:T(8,128)(2,1)}, u32[]{:S(2)}, u32[]{:S(2)}) collective-permute-start(bf16[4,576,128]{2,1,0:T(8,128)(2,1)} %constant_dynamic-update-slice_fusion), channel_id=1, source_target_pairs={{0,1},{1,2},{2,3},{3,4},{4,5},{5,6},{6,7},{7,8},{8,9},{9,10},{10,1... | collective-permute-start | bytes 1769480 | tf_op jit(solution)/shard_map/ppermute | solution.py:322
  208.2 1.4 copy-start.1
  209.6 0.8 copy-start.5
  210.4 0.8 copy-start.7
  211.3 0.9 copy-start.11
  212.2 0.8 copy-start.14
  212.9 0.8 copy-start.17
  213.7 21.0 %copy-start.3 = (bf16[4,384,128]{2,1,0:T(8,128)(2,1)S(1)}, bf16[4,384,128]{2,1,0:T(8,128)(2,1)}, u32[]{:S(2)}) copy-start(bf16[4,384,128]{2,1,0:T(8,128)(2,1)} %copy-done.2) | copy-start | bytes 1179652
  213.7 21.0 %copy-start.9 = (bf16[4,192,128]{2,1,0:T(8,128)(2,1)S(1)}, bf16[4,192,128]{2,1,0:T(8,128)(2,1)}, u32[]{:S(2)}) copy-start(bf16[4,192,128]{2,1,0:T(8,128)(2,1)} %copy-done.8) | copy-start | bytes 589828
  228.8 8.2 %copy-start.12 = (s32[80,256]{1,0:T(8,128)S(1)}, s32[80,256]{1,0:T(8,128)}, u32[]{:S(2)}) copy-start(s32[80,256]{1,0:T(8,128)} %constant.6.clone.refs_11_) | copy-start | bytes 245764
  228.8 8.2 %copy-start.15 = (s32[10,80,4]{2,1,0:T(8,128)S(1)}, s32[10,80,4]{2,1,0:T(8,128)}, u32[]{:S(2)}) copy-start(s32[10,80,4]{2,1,0:T(8,128)} %add_bitcast_fusion.refs_9_) | copy-start | bytes 38404
  228.8 8.2 %copy-start.18 = (bf16[2,128,128]{2,1,0:T(8,128)(2,1)S(1)}, bf16[2,128,128]{2,1,0:T(8,128)(2,1)}, u32[]{:S(2)}) copy-start(bf16[2,128,128]{2,1,0:T(8,128)(2,1)} %get-tuple-element.23) | copy-start | bytes 196612
  228.8 8.2 %copy-start.19 = (bf16[2,128,128]{2,1,0:T(8,128)(2,1)S(1)}, bf16[2,128,128]{2,1,0:T(8,128)(2,1)}, u32[]{:S(2)}) copy-start(bf16[2,128,128]{2,1,0:T(8,128)(2,1)} %get-tuple-element.24) | copy-start | bytes 196612
  228.8 8.2 %copy-start.21 = (bf16[128,128]{1,0:T(8,128)(2,1)S(1)}, bf16[128,128]{1,0:T(8,128)(2,1)}, u32[]{:S(2)}) copy-start(bf16[128,128]{1,0:T(8,128)(2,1)} %slice_bitcast_fusion.refs_14_) | copy-start | bytes 98308
  228.9 8.2 %copy-start.23 = (f32[128]{0:T(128)S(1)}, f32[128]{0:T(128)}, u32[]{:S(2)}) copy-start(f32[128]{0:T(128)} %param.23) | copy-start | bytes 1540
  228.9 5.9 %collective-permute-start.7 = (bf16[4,64,128]{2,1,0:T(8,128)(2,1)S(1)}, bf16[4,64,128]{2,1,0:T(8,128)(2,1)S(1)}, u32[]{:S(2)}, u32[]{:S(2)}) collective-permute-start(bf16[4,64,128]{2,1,0:T(8,128)(2,1)S(1)} %get-tuple-element.16), channel_id=1, source_target_pairs={{1,0},{2,1},{3,2},{4,3},{5,4},{6,5},{7,6},{8,7},{9,8},{10,9},{11,1... | collective-permute-start | bytes 196616 | tf_op jit(solution)/shard_map/ppermute | solution.py:323
  230.3 5.6 %collective-permute-start.5 = (bf16[4,64,128]{2,1,0:T(8,128)(2,1)S(1)}, bf16[4,64,128]{2,1,0:T(8,128)(2,1)S(1)}, u32[]{:S(2)}, u32[]{:S(2)}) collective-permute-start(bf16[4,64,128]{2,1,0:T(8,128)(2,1)S(1)} %get-tuple-element.16), channel_id=1, source_target_pairs={{0,1},{1,2},{2,3},{3,4},{4,5},{5,6},{6,7},{7,8},{8,9},{9,10},{10,1... | collective-permute-start | bytes 196616 | tf_op jit(solution)/shard_map/ppermute | solution.py:322

commit v3 on v2

--- a/solution.py
+++ b/solution.py
@@ -124,7 +124,7 @@
             sums[...] += jnp.sum(res.astype(jnp.float32).reshape(-1, 8, 128), axis=0)
 
 
-def layer(name, main, top, bottom, origin, codes, outer, weights, bias, first, count, pool, canvas=None):
+def layer(name, main, top, bottom, origin, codes, outer, skip, weights, bias, first, count, pool, canvas=None):
     rows, cols, width = main.shape
     total = cols // USE
     held = top.shape[1] // EDGE
@@ -153,7 +153,7 @@
         [spec(rows, lambda w: first + w, USE), spec(rows, left_of, EDGE), spec(rows, right_of, EDGE)]
         + halo + halo
         + [pl.BlockSpec((1, WIN, rows), lambda w: (first + w, 0, 0))]
-        + [pl.BlockSpec((1, WIN, 2 * DEEP), lambda w: (first + w, 0, 0))]
+        + [pl.BlockSpec((1, WIN, 2 * DEEP), lambda w: (skip + first + w, 0, 0))]
         + [whole(WIN, 256), whole(256, 128), whole(256, 128), whole(128, 128), whole(1, 128)]
     )
     operands = [main] * 3 + [top] * 3 + [bottom] * 3 + [codes, outer, jnp.asarray(bit_table())]
@@ -276,7 +276,7 @@
     )(part)
 
 
-SPLITS = (0.3, 0.9, 1.0)
+SPLITS = (0.15, 0.45, 0.92, 1.0)
 
 
 def on_device(features, links, coarse_links, fine_weight, fine_bias, coarse_weight, coarse_bias):
@@ -285,46 +285,47 @@
     total = cols // USE
     ends = [round(total * f) for f in SPLITS]
     starts = [0] + ends[:-1]
-    split = ends[0] * USE
-    near = (DEEP, split + USE, width)
+    near = (DEEP, (ends[0] + 1) * USE, width)
     lines = near[0] * near[1]
-    fine_lines = DEEP * cols * 2 // 128
+    all_cols = cols + coarse_links.shape[1]
 
     def exchanged(pick, coarse_pick):
-        return jnp.concatenate(
-            [features[pick, : split + USE].reshape(-1, 128), coded(links[pick]), coded(coarse_links[coarse_pick])]
-        )
+        codes = jnp.concatenate([links[pick], coarse_links[coarse_pick]], axis=1)
+        return jnp.concatenate([features[pick, : near[1]].reshape(-1, 128), coded(codes)])
 
     last, start = slice(rows - DEEP, rows), slice(0, DEEP)
     coarse_rows = coarse_links.shape[0]
     above = lax.ppermute(exchanged(last, slice(coarse_rows - DEEP, coarse_rows)), "tile", up)
     below = lax.ppermute(exchanged(start, start), "tile", down)
-    far_above = lax.ppermute(features[last, split - USE :], "tile", up)
-    far_below = lax.ppermute(features[start, split - USE :], "tile", down)
-    fine_codes = code_windows(links)
-    coarse_codes = code_windows(coarse_links)
-    ghosts = [decoded(part[lines : lines + fine_lines], (DEEP, cols)) for part in (above, below)]
-    fine_outer = code_windows(jnp.concatenate(ghosts))
-    ghosts = [decoded(part[lines + fine_lines :], (DEEP, cols // 4)) for part in (above, below)]
-    coarse_outer = code_windows(jnp.concatenate(ghosts))
     halos = [(above[:lines].reshape(near), below[:lines].reshape(near), 0)]
-    halos += [(far_above, far_below, ends[0] - 1)] * (len(ends) - 1)
+
+    def further(lo, hi, after):
+        pair = (features[last, lo * USE : hi * USE], features[start, lo * USE : hi * USE])
+        pair, _ = lax.optimization_barrier((pair, after))
+        return lax.ppermute(pair[0], "tile", up), lax.ppermute(pair[1], "tile", down), lo
+
+    halos.append(further(ends[0] - 1, ends[1] + 1, (above, below)))
+    fine_codes, coarse_codes = lax.optimization_barrier((code_windows(links), code_windows(coarse_links)))
+    ghosts = [decoded(part[lines:], (DEEP, all_cols)) for part in (above, below)]
+    outer = code_windows(jnp.concatenate(ghosts))
     canvas = None
     mids, tops, bottoms = [], [], []
     for n, (lo, hi) in enumerate(zip(starts, ends)):
         canvas, mid = layer(
-            f"fine{n}", features, *halos[n], fine_codes, fine_outer, fine_weight, fine_bias, lo, hi - lo, True, canvas
+            f"fine{n}", features, *halos[n], fine_codes, outer, 0, fine_weight, fine_bias, lo, hi - lo, True, canvas
         )
         mids.append(mid)
         if n == 0:
+            halos += [further(ends[1] - 1, total, (mid, halos[1][0], halos[1][1]))] * 2
+        if n < 2:
             continue
-        send = jnp.concatenate(mids[:2], axis=1) if n == 1 else mid
+        send = jnp.concatenate(mids, axis=1) if n == 2 else mid
         tops.append(lax.ppermute(send, "tile", up))
         bottoms.append(lax.ppermute(send, "tile", down))
     coarse_in = jnp.concatenate(mids, axis=1)
     coarse_map, sums = layer(
         "coarse", coarse_in, jnp.concatenate(tops, axis=1), jnp.concatenate(bottoms, axis=1), 0,
-        coarse_codes, coarse_outer, coarse_weight, coarse_bias, 0, coarse_in.shape[1] // USE, False,
+        coarse_codes, outer, total, coarse_weight, coarse_bias, 0, coarse_in.shape[1] // USE, False,
     )
     real_count = jnp.sum((coarse_links >> 8 & 1).astype(jnp.float32))
     pooled = total_over_tiles(jnp.concatenate([sums, jnp.broadcast_to(real_count, (8, 128))]))

time: 268 us -> 250 us (0.933)
  starting transfers between devices: 44.3 us -> 27.6 us
  Pallas kernels: 164 us -> 171 us
  other arithmetic: 14.9 us -> 10.3 us
  local copies, waits for them, and re-layouts: 41.4 us -> 38.4 us
    ppermute x2, starting transfers between devices: 29.4 us -> 9.07 us  [on_device(): tops.append(lax.ppermute(send, 'tile', up))]
    ppermute x2 -> x4, starting transfers between devices: 7.45 us -> 12.2 us  [the longest x2 9.48 us: further(): lax.ppermute(pair[0], 'tile', up)]
    unnamed x62 -> x41, local copies, waits for them, and re-layouts: 11.8 us -> 7.57 us
    pallas_call x1, Pallas kernels: 12.2 us -> 16.1 us  [total_over_tiles(): pl.pallas_call(lambda *refs: total_kernel(size, *refs), in_specs=[pl.Bloc...]
    add x10 -> x6, local copies, waits for them, and re-layouts: 8.89 us -> 11.2 us  [decoded(): return pair[0] + 256 * pair[1]]
    pallas_call x4 -> x5, Pallas kernels: 152 us -> 154 us  [layer(): pl.pallas_call(lambda *refs: window_kernel(rows, pool, refs), grid=(count...]
    slice x2 -> x3, local copies, waits for them, and re-layouts: 5.82 us -> 7.8 us  [the longest x2 6.54 us: further(): features[start, lo * USE:hi * USE]]
  transfers between devices with their start and end apart: 8 -> 10, of which waited for: 0 -> 1; matrix products, arithmetic and copies ran while one was open for 15% -> 17% of each run, Pallas kernels for 21% -> 30%
where the time goes in v3:
time: 250 us; the launch traced here: 249 us
  Pallas kernels  171 us (68%)
  local copies, waits for them, and re-layouts  38.4 us (15%)
  starting transfers between devices  27.6 us (11%)
  other arithmetic  10.3 us (4%)
    pallas_call x5, Pallas kernels, layer(): pl.pallas_call(lambda *refs: window_kernel(rows, pool, refs), grid=(count...  154 us
    pallas_call x1, Pallas kernels, total_over_tiles(): pl.pallas_call(lambda *refs: total_kernel(size, *refs), in_specs=[pl.Bloc...  16.1 us
    add x6, local copies, waits for them, and re-layouts, decoded(): return pair[0] + 256 * pair[1]  11.2 us
    ppermute x2, starting transfers between devices, further(): lax.ppermute(pair[0], 'tile', up)  9.48 us
    ppermute x2, starting transfers between devices, on_device(): tops.append(lax.ppermute(send, 'tile', up))  9.07 us
    unnamed x41, local copies, waits for them, and re-layouts  7.57 us
    slice x2, local copies, waits for them, and re-layouts, further(): features[start, lo * USE:hi * USE]  6.54 us
  transfers between devices with their start and end apart: 10, of which 1 were waited for; matrix products, arithmetic and copies ran while one was open for 17% of the time, Pallas kernels for 30%

profile of v3, /device:TPU:0, one launch (start us, length us, event | category | flops | bytes accessed | tf_op | source)
XLA Modules:
  0.0 248.7 jit_solution(2935281081005806333)
XLA Ops:
  0.6 0.9 slice_bitcast_fusion
  1.6 0.7 and_convert_fusion
  2.3 0.1 pad_maximum_fusion.5
  2.5 1.3 fusion.3
  3.7 0.8 pad_maximum_fusion.3
  4.6 2.4 collective-permute-start
  7.0 0.8 pad_maximum_fusion.4
  7.8 1.3 collective-permute-start.1
  9.1 0.1 fusion.7
  9.2 0.1 reshape.239
  9.3 0.1 fusion.8
  9.4 0.2 copy.76
  9.6 0.6 fusion.6
  10.2 0.6 slice_bitcast_fusion.3.refs_14_
  10.8 3.7 %fusion.4 = (bf16[4,1472,128]{2,1,0:T(8,128)(2,1)}, bf16[4,1472,128]{2,1,0:T(8,128)(2,1)}) fusion(bf16[16,2560,128]{2,1,0:T(8,128)(2,1)} %refs_2_.7), kind=kLoop, calls=%fused_computation.34 | loop fusion | bytes 6029312 | tf_op jit(solution)/shard_map/slice | solution.py:303
  14.5 0.1 pad.26
  14.6 0.1 reshape.241
  14.7 0.1 slice.152
  14.9 0.1 reshape.240
  15.0 0.2 copy.81
  15.2 0.2 copy.82
  15.4 0.8 add_bitcast_fusion.1.refs_9_
  16.2 2.9 %fusion.2 = (bf16[4,896,128]{2,1,0:T(8,128)(2,1)}, bf16[4,896,128]{2,1,0:T(8,128)(2,1)}) fusion(bf16[16,2560,128]{2,1,0:T(8,128)(2,1)} %refs_2_.7), kind=kLoop, calls=%fused_computation.32 | loop fusion | bytes 3670016 | tf_op jit(solution)/shard_map/slice | solution.py:303
  19.1 0.2 pad_add_fusion
  19.3 0.5 copy.68
  19.9 0.7 fusion.1
  20.7 0.7 copy-done.13
  21.4 5.2 %collective-permute-start.2 = (bf16[4,896,128]{2,1,0:T(8,128)(2,1)}, bf16[4,896,128]{2,1,0:T(8,128)(2,1)S(1)}, u32[]{:S(2)}, u32[]{:S(2)}) collective-permute-start(bf16[4,896,128]{2,1,0:T(8,128)(2,1)} %get-tuple-element.21), channel_id=1, source_target_pairs={{0,1},{1,2},{2,3},{3,4},{4,5},{5,6},{6,7},{7,8},{8,9},{9,10},{10,1... | collective-permute-start | bytes 2752520 | tf_op jit(solution)/shard_map/ppermute | solution.py:305
  26.6 1.3 collective-permute-start.3
  27.9 0.8 slice_convert_fusion
  28.7 0.6 fusion
  29.3 1.4 add.38
  30.8 1.5 add.35
  32.3 1.5 add.39
  33.7 1.5 add.37
  35.3 1.6 slice_add_fusion
  36.9 2.5 %copy.83 = s32[8,3136]{0,1:T(8,128)} copy(s32[8,3136]{1,0:T(8,128)} %get-tuple-element.49) | data formatting | bytes 200704
  39.5 1.5 pad.29.clone
  41.0 0.7 slice.163
  41.7 2.5 %copy.84 = s32[8,3136]{0,1:T(8,128)} copy(s32[8,3136]{1,0:T(8,128)} %get-tuple-element.50) | data formatting | bytes 200704
  44.2 1.5 pad.30.clone
  45.8 0.7 slice.164
  46.5 2.7 %copy.72 = s32[4,50,64]{0,2,1:T(8,128)} copy(s32[4,50,64]{2,1,0:T(8,128)} %add.35) | data formatting | bytes 102400 | tf_op jit(solution)/shard_map/add | solution.py:220
  49.2 2.6 %copy.73 = s32[4,50,64]{0,2,1:T(8,128)} copy(s32[4,50,64]{2,1,0:T(8,128)} %add.37) | data formatting | bytes 102400 | tf_op jit(solution)/shard_map/add | solution.py:220
  51.8 1.2 slice.149
  53.0 1.1 slice.150
  54.1 2.2 add_bitcast_fusion.refs_10_
  56.4 21.8 %fine0.1 = (bf16[16,2560,128]{2,1,0:T(8,128)(2,1)}, bf16[4,96,128]{2,1,0:T(8,128)(2,1)S(1)}) custom-call(bf16[16,2560,128]{2,1,0:T(8,128)(2,1)} %refs_2_.7, bf16[16,2560,128]{2,1,0:T(8,128)(2,1)} %refs_2_.7, bf16[16,2560,128]{2,1,0:T(8,128)(2,1)} %refs_2_.7, bf16[4,448,128]{2,1,0:T(8,128)(2,1)S(1)} %bitcast.35, bf16[4,448,128]{2,1,0:T(8,128)(2,1)S(1)} %bitcast.36, ...), custom_call_target="tpu_custom_call" | custom-call | flops 3019898880 | bytes 5898240 | tf_op jit(solution)/shard_map/fine0/pallas_call | solution.py:181
  78.2 4.3 %collective-permute-start.4 = (bf16[4,1472,128]{2,1,0:T(8,128)(2,1)S(1)}, bf16[4,1472,128]{2,1,0:T(8,128)(2,1)S(1)}, u32[]{:S(2)}, u32[]{:S(2)}) collective-permute-start(bf16[4,1472,128]{2,1,0:T(8,128)(2,1)S(1)} %copy-done.11), channel_id=1, source_target_pairs={{0,1},{1,2},{2,3},{3,4},{4,5},{5,6},{6,7},{7,8},{8,9},{9,10},{10,1... | collective-permute-start | bytes 4521992 | tf_op jit(solution)/shard_map/ppermute | solution.py:305
  82.6 1.5 collective-permute-start.5
  84.1 41.6 %fine1.1 = (bf16[16,2560,128]{2,1,0:T(8,128)(2,1)}, bf16[4,192,128]{2,1,0:T(8,128)(2,1)S(1)}) custom-call(bf16[16,2560,128]{2,1,0:T(8,128)(2,1)} %refs_2_.7, bf16[16,2560,128]{2,1,0:T(8,128)(2,1)} %refs_2_.7, bf16[16,2560,128]{2,1,0:T(8,128)(2,1)} %refs_2_.7, ...), custom_call_target="tpu_custom_call", output_to_operand_aliasing={{0}: (18, {})} | custom-call | flops 6039797760 | bytes 11796480 | tf_op jit(solution)/shard_map/fine1/pallas_call | solution.py:181
  125.7 64.8 %fine2.1 = (bf16[16,2560,128]{2,1,0:T(8,128)(2,1)}, bf16[4,304,128]{2,1,0:T(8,128)(2,1)S(1)}) custom-call(bf16[16,2560,128]{2,1,0:T(8,128)(2,1)} %refs_2_.7, bf16[16,2560,128]{2,1,0:T(8,128)(2,1)} %refs_2_.7, bf16[16,2560,128]{2,1,0:T(8,128)(2,1)} %refs_2_.7, ...), custom_call_target="tpu_custom_call", output_to_operand_aliasing={{0}: (18, {})} | custom-call | flops 9563013120 | bytes 18677760 | tf_op jit(solution)/shard_map/fine2/pallas_call | solution.py:181
  190.5 1.3 collective-permute-start.8
  191.8 0.6 convert_reduce_fusion
  192.4 4.8 %collective-permute-start.6 = (bf16[4,592,128]{2,1,0:T(8,128)(2,1)S(1)}, bf16[4,592,128]{2,1,0:T(8,128)(2,1)S(1)}, u32[]{:S(2)}, u32[]{:S(2)}) collective-permute-start(bf16[4,592,128]{2,1,0:T(8,128)(2,1)S(1)} %constant_dynamic-update-slice_fusion), channel_id=1, source_target_pairs={{0,1},{1,2},{2,3},{3,4},{4,5},{5,6},{6,7},{7,8},{8,9},{9,10},{10,1... | collective-permute-start | bytes 1818632 | tf_op jit(solution)/shard_map/ppermute | solution.py:323
  197.3 11.8 %fine3.1 = (bf16[16,2560,128]{2,1,0:T(8,128)(2,1)}, bf16[4,48,128]{2,1,0:T(8,128)(2,1)S(1)}) custom-call(bf16[16,2560,128]{2,1,0:T(8,128)(2,1)} %refs_2_.7, bf16[16,2560,128]{2,1,0:T(8,128)(2,1)} %refs_2_.7, bf16[16,2560,128]{2,1,0:T(8,128)(2,1)} %refs_2_.7, ...), custom_call_target="tpu_custom_call", output_to_operand_aliasing={{0}: (18, {})} | custom-call | flops 1509949440 | bytes 2949120 | tf_op jit(solution)/shard_map/fine3/pallas_call | solution.py:181
  209.1 1.3 collective-permute-start.9
  210.3 4.2 %collective-permute-start.7 = (bf16[4,48,128]{2,1,0:T(8,128)(2,1)S(1)}, bf16[4,48,128]{2,1,0:T(8,128)(2,1)S(1)}, u32[]{:S(2)}, u32[]{:S(2)}) collective-permute-start(bf16[4,48,128]{2,1,0:T(8,128)(2,1)S(1)} %get-tuple-element.31), channel_id=1, source_target_pairs={{0,1},{1,2},{2,3},{3,4},{4,5},{5,6},{6,7},{7,8},{8,9},{9,10},{10,1... | collective-permute-start | bytes 147464 | tf_op jit(solution)/shard_map/ppermute | solution.py:323
  214.7 0.7 collective-permute-done.7
  215.5 0.1 copy-done.4
  215.6 14.5 %coarse.1 = (bf16[4,640,128]{2,1,0:T(8,128)(2,1)}, f32[8,128]{1,0:T(8,128)S(1)}) custom-call(bf16[4,640,128]{2,1,0:T(8,128)(2,1)S(1)} %pad_maximum_fusion.refs_0_.refs_1_.refs_2_, bf16[4,640,128]{2,1,0:T(8,128)(2,1)S(1)} %pad_maximum_fusion.refs_0_.refs_1_.refs_2_, bf16[4,640,128]{2,1,0:T(8,128)(2,1)S(1)} %pad_maximum_fusion.refs_0_.refs_1_.refs_2_, ...), custom_call_target="tpu_custom_call" | custom-call | flops 2516582400 | bytes 4915200 | tf_op jit(solution)/shard_map/coarse/pallas_call | solution.py:181
  230.2 1.2 concatenate.92.refs_0_
  231.4 16.1 %total.1 = f32[1,128]{1,0:T(1,128)} custom-call(f32[16,128]{1,0:T(8,128)} %concatenate.92.refs_0_), custom_call_target="tpu_custom_call" | custom-call | tf_op jit(solution)/shard_map/total/pallas_call | solution.py:264
  247.6 1.1 copy.91
  (57 shorter events, 0.5 us)
Async XLA Ops:
  2.4 6.7 %copy-start.9 = (s32[16,2560]{1,0:T(8,128)S(1)}, s32[16,2560]{1,0:T(8,128)}, u32[]{:S(2)}) copy-start(s32[16,2560]{1,0:T(8,128)} %param.21) | copy-start | bytes 491524
  3.7 5.6 %copy-start.14 = (s32[4,640]{1,0:T(4,128)S(1)}, s32[4,640]{1,0:T(4,128)}, u32[]{:S(2)}) copy-start(s32[4,640]{1,0:T(4,128)} %param.22) | copy-start | bytes 30724
  3.7 5.9 %copy-start.15 = (bf16[5,128,128]{2,1,0:T(8,128)(2,1)S(1)}, bf16[5,128,128]{2,1,0:T(8,128)(2,1)}, u32[]{:S(2)}) copy-start(bf16[5,128,128]{2,1,0:T(8,128)(2,1)} %param.23) | copy-start | bytes 491524
  4.6 15.3 %collective-permute-start = (bf16[1992,128]{1,0:T(8,128)(2,1)}, bf16[1992,128]{1,0:T(8,128)(2,1)S(1)}, u32[]{:S(2)}, u32[]{:S(2)}) collective-permute-start(bf16[1992,128]{1,0:T(8,128)(2,1)} %pad_maximum_fusion.3), channel_id=1, source_target_pairs={{0,1},{1,2},{2,3},{3,4},{4,5},{5,6},{6,7},{7,8},{8,9},{9,10},{10,1... | collective-permute-start | bytes 1529864 | tf_op jit(solution)/shard_map/ppermute | solution.py:298
  7.8 12.8 %collective-permute-start.1 = (bf16[1992,128]{1,0:T(8,128)(2,1)}, bf16[1992,128]{1,0:T(8,128)(2,1)S(1)}, u32[]{:S(2)}, u32[]{:S(2)}) collective-permute-start(bf16[1992,128]{1,0:T(8,128)(2,1)} %pad_maximum_fusion.4), channel_id=1, source_target_pairs={{1,0},{2,1},{3,2},{4,3},{5,4},{6,5},{7,6},{8,7},{9,8},{10,9},{11,1... | collective-permute-start | bytes 1529864 | tf_op jit(solution)/shard_map/ppermute | solution.py:299
  19.8 0.8 copy-start.12
  20.6 0.8 copy-start.13
  21.4 56.9 %collective-permute-start.2 = (bf16[4,896,128]{2,1,0:T(8,128)(2,1)}, bf16[4,896,128]{2,1,0:T(8,128)(2,1)S(1)}, u32[]{:S(2)}, u32[]{:S(2)}) collective-permute-start(bf16[4,896,128]{2,1,0:T(8,128)(2,1)} %get-tuple-element.21), channel_id=1, source_target_pairs={{0,1},{1,2},{2,3},{3,4},{4,5},{5,6},{6,7},{7,8},{8,9},{9,10},{10,1... | collective-permute-start | bytes 2752520 | tf_op jit(solution)/shard_map/ppermute | solution.py:305
  26.6 51.7 %collective-permute-start.3 = (bf16[4,896,128]{2,1,0:T(8,128)(2,1)}, bf16[4,896,128]{2,1,0:T(8,128)(2,1)S(1)}, u32[]{:S(2)}, u32[]{:S(2)}) collective-permute-start(bf16[4,896,128]{2,1,0:T(8,128)(2,1)} %get-tuple-element.22), channel_id=1, source_target_pairs={{1,0},{2,1},{3,2},{4,3},{5,4},{6,5},{7,6},{8,7},{9,8},{10,9},{11,1... | collective-permute-start | bytes 2752520 | tf_op jit(solution)/shard_map/ppermute | solution.py:305
  51.8 2.2 copy-start.8
  54.0 2.3 copy-start
  54.0 2.3 copy-start.1
  54.1 2.3 copy-start.2
  54.1 2.3 copy-start.3
  54.1 2.3 copy-start.5
  54.1 2.3 copy-start.6
  56.4 21.8 %copy-start.11 = (bf16[4,1472,128]{2,1,0:T(8,128)(2,1)S(1)}, bf16[4,1472,128]{2,1,0:T(8,128)(2,1)}, u32[]{:S(2)}) copy-start(bf16[4,1472,128]{2,1,0:T(8,128)(2,1)} %get-tuple-element.23) | copy-start | bytes 4521988
  56.4 26.2 %copy-start.10 = (bf16[4,1472,128]{2,1,0:T(8,128)(2,1)S(1)}, bf16[4,1472,128]{2,1,0:T(8,128)(2,1)}, u32[]{:S(2)}) copy-start(bf16[4,1472,128]{2,1,0:T(8,128)(2,1)} %get-tuple-element.24) | copy-start | bytes 4521988
  56.4 27.6 %copy-start.16 = (bf16[5,128,128]{2,1,0:T(8,128)(2,1)S(1)}, bf16[5,128,128]{2,1,0:T(8,128)(2,1)}, u32[]{:S(2)}) copy-start(bf16[5,128,128]{2,1,0:T(8,128)(2,1)} %param.25) | copy-start | bytes 491524
  78.2 47.5 %collective-permute-start.4 = (bf16[4,1472,128]{2,1,0:T(8,128)(2,1)S(1)}, bf16[4,1472,128]{2,1,0:T(8,128)(2,1)S(1)}, u32[]{:S(2)}, u32[]{:S(2)}) collective-permute-start(bf16[4,1472,128]{2,1,0:T(8,128)(2,1)S(1)} %copy-done.11), channel_id=1, source_target_pairs={{0,1},{1,2},{2,3},{3,4},{4,5},{5,6},{6,7},{7,8},{8,9},{9,10},{10,1... | collective-permute-start | bytes 4521992 | tf_op jit(solution)/shard_map/ppermute | solution.py:305
  82.6 43.1 %collective-permute-start.5 = (bf16[4,1472,128]{2,1,0:T(8,128)(2,1)S(1)}, bf16[4,1472,128]{2,1,0:T(8,128)(2,1)S(1)}, u32[]{:S(2)}, u32[]{:S(2)}) collective-permute-start(bf16[4,1472,128]{2,1,0:T(8,128)(2,1)S(1)} %copy-done.10), channel_id=1, source_target_pairs={{1,0},{2,1},{3,2},{4,3},{5,4},{6,5},{7,6},{8,7},{9,8},{10,9},{11,1... | collective-permute-start | bytes 4521992 | tf_op jit(solution)/shard_map/ppermute | solution.py:305
  190.5 24.2 %collective-permute-start.8 = (bf16[4,592,128]{2,1,0:T(8,128)(2,1)S(1)}, bf16[4,592,128]{2,1,0:T(8,128)(2,1)S(1)}, u32[]{:S(2)}, u32[]{:S(2)}) collective-permute-start(bf16[4,592,128]{2,1,0:T(8,128)(2,1)S(1)} %constant_dynamic-update-slice_fusion), channel_id=1, source_target_pairs={{1,0},{2,1},{3,2},{4,3},{5,4},{6,5},{7,6},{8,7},{9,8},{10,9},{11,1... | collective-permute-start | bytes 1818632 | tf_op jit(solution)/shard_map/ppermute | solution.py:324
  192.4 23.0 %collective-permute-start.6 = (bf16[4,592,128]{2,1,0:T(8,128)(2,1)S(1)}, bf16[4,592,128]{2,1,0:T(8,128)(2,1)S(1)}, u32[]{:S(2)}, u32[]{:S(2)}) collective-permute-start(bf16[4,592,128]{2,1,0:T(8,128)(2,1)S(1)} %constant_dynamic-update-slice_fusion), channel_id=1, source_target_pairs={{0,1},{1,2},{2,3},{3,4},{4,5},{5,6},{6,7},{7,8},{8,9},{9,10},{10,1... | collective-permute-start | bytes 1818632 | tf_op jit(solution)/shard_map/ppermute | solution.py:323
  209.1 5.6 %collective-permute-start.9 = (bf16[4,48,128]{2,1,0:T(8,128)(2,1)S(1)}, bf16[4,48,128]{2,1,0:T(8,128)(2,1)S(1)}, u32[]{:S(2)}, u32[]{:S(2)}) collective-permute-start(bf16[4,48,128]{2,1,0:T(8,128)(2,1)S(1)} %get-tuple-element.31), channel_id=1, source_target_pairs={{1,0},{2,1},{3,2},{4,3},{5,4},{6,5},{7,6},{8,7},{9,8},{10,9},{11,1... | collective-permute-start | bytes 147464 | tf_op jit(solution)/shard_map/ppermute | solution.py:324
  210.3 5.1 %collective-permute-start.7 = (bf16[4,48,128]{2,1,0:T(8,128)(2,1)S(1)}, bf16[4,48,128]{2,1,0:T(8,128)(2,1)S(1)}, u32[]{:S(2)}, u32[]{:S(2)}) collective-permute-start(bf16[4,48,128]{2,1,0:T(8,128)(2,1)S(1)} %get-tuple-element.31), channel_id=1, source_target_pairs={{0,1},{1,2},{2,3},{3,4},{4,5},{5,6},{6,7},{7,8},{8,9},{9,10},{10,1... | collective-permute-start | bytes 147464 | tf_op jit(solution)/shard_map/ppermute | solution.py:323
  214.6 1.0 copy-start.4
  214.6 1.0 copy-start.7
